TPU v7x, 32 devices: a whole 2x2x4 slice. The times are simulated.
32 devices in a mesh: band: 8 (over z, y), mp: 4 (over x, core).
Axes of the slice: x: 2, y: 2, z: 4, core: 2. Of those that a mesh axis runs over, the one named last changes fastest.
Arguments:
- cells: bfloat16 [2048, 1024], P('band', 'mp'), may hold values from -81 to 81
- row_gain: float32 [1024], replicated, may hold values from 0.1 to 1.9
- row_qkv: bfloat16 [3, 1024, 1024], P(None, None, 'mp'), may hold values from -1.25 to 1.25
- row_out: bfloat16 [1024, 1024], P('mp'), may hold values from -0.1875 to 0.1875
- col_gain: float32 [1024], replicated, may hold values from 0.1 to 1.9
- col_qkv: bfloat16 [3, 1024, 1024], P(None, None, 'mp'), may hold values from -1.25 to 1.25
- col_out: bfloat16 [1024, 1024], P('mp'), may hold values from -0.1875 to 0.1875
- row_seg: int32 [2048], P('band'), may hold values from 0 to 255, never falling along the last dimension, each value on 1 to 16 neighbouring positions
- col_dest: int32 [2048, 1], P('band'), may hold values from 0 to 7; in each aligned block of 256 rows (0 to 255, 256 to 511, ...) at most 48 rows name the same one
- sheet_column_index: int32 [2048], P('band'), may hold values from 1 to 8
- d_result: bfloat16 [2048, 1024], P('band', 'mp'), may hold values from -6 to 6
Outputs:
- result: bfloat16 [2048, 1024], P('band', 'mp')
- d_cells: bfloat16 [2048, 1024], P('band', 'mp')
Inputs may be any that keep to these rules, and one draw needn't show every extreme that they name: `row_seg`: cells never fall in value along the array. `col_dest`: at most 48 of the cells of one row band name the same column band, and some row band sends exactly 48 to some column band.
All inputs are finite; a program needn't handle non-finite values.
Results may differ from a plain program's by a relative error of at most 0.019.
Values may be sent and summed in bfloat16 or wider, within the bound.
A program may use at most 64 MiB of HBM per device.

v0:
```python
import jax
import jax.numpy as jnp
from jax import lax
from jax.sharding import PartitionSpec as P

HEAD_DIM = 64
TILE = 128


norm_eps = 1e-06
neg_fill = -1e30


def block_terms(inputs, norm_gain, query_key_value_weight, w_out, allowed, tile_rows):
    values = inputs.astype(jnp.float32)
    inv_rms = lax.rsqrt(jnp.mean(values * values, axis=-1, keepdims=True) + norm_eps)
    normalized_cells = (values * inv_rms * norm_gain).astype(jnp.bfloat16)
    projected_heads = jnp.einsum(
        "lu,xuh->xlh", normalized_cells, query_key_value_weight, preferred_element_type=jnp.float32
    ).astype(jnp.bfloat16)
    row_count = inputs.shape[0]
    feat_width = query_key_value_weight.shape[2]
    head_count = feat_width // HEAD_DIM
    shaped = projected_heads.reshape(3, row_count // tile_rows, tile_rows, head_count, HEAD_DIM)
    scores = jnp.einsum(
        "bqhe,bkhe->bhqk", shaped[0], shaped[1], preferred_element_type=jnp.float32
    ) * HEAD_DIM ** (-0.5)
    scores = jnp.where(allowed[:, None], scores, neg_fill)
    scores = scores - lax.stop_gradient(jnp.max(scores, axis=-1, keepdims=True))
    expd = jnp.exp(scores)
    attn_probs = (expd / jnp.sum(expd, axis=-1, keepdims=True)).astype(jnp.bfloat16)
    attended = jnp.einsum(
        "bhqk,bkhe->bqhe", attn_probs, shaped[2], preferred_element_type=jnp.float32
    ).astype(jnp.bfloat16)
    attended = attended.reshape(row_count, feat_width)
    return jnp.dot(attended, w_out, preferred_element_type=jnp.float32)


def column_band_mask(col_keys):
    positions = jnp.arange(col_keys.shape[0])
    same_col = (col_keys[:, None] == col_keys[None, :]) & (col_keys[None, :] > 0)
    return (same_col | (positions[:, None] == positions[None, :]))[None]


def widen(block):
    return lax.all_gather(block, "mp", axis=1, tiled=True)


def narrow(terms):
    return lax.psum_scatter(
        terms.astype(jnp.bfloat16), "mp", scatter_dimension=1, tiled=True
    ).astype(jnp.float32)


def move_rows(rows):
    return lax.all_to_all(rows, "band", split_axis=0, concat_axis=0, tiled=True)


def on_device(
    cells,
    row_gain,
    row_qkv,
    row_out,
    col_gain,
    col_qkv,
    col_out,
    row_seg,
    col_dest,
    sheet_column_index,
    d_result,
):
    cell_rows, feat_width = cells.shape
    band_count = lax.axis_size("band")
    capacity = max(2, 3 * cell_rows // (2 * band_count))
    slot_total = band_count * capacity
    gathered = widen(cells)
    row_groups = row_seg.reshape(cell_rows // TILE, TILE)
    row_mask = row_groups[:, :, None] == row_groups[:, None, :]

    def row_local(inputs):
        return block_terms(inputs, row_gain, row_qkv, row_out, row_mask, TILE)

    row_terms, row_pull = jax.vjp(row_local, gathered)
    target = col_dest[:, 0]
    onehot = (target[:, None] == jnp.arange(band_count, dtype=jnp.int32)[None, :]).astype(jnp.int32)
    ranking = jnp.sum((jnp.cumsum(onehot, axis=0) - onehot) * onehot, axis=1)
    slot_index = target * capacity + ranking
    keys_out = (
        jnp.zeros((slot_total,), jnp.bfloat16)
        .at[slot_index]
        .set(sheet_column_index.astype(jnp.bfloat16))
    )
    back_in = jnp.zeros((slot_total, feat_width), jnp.bfloat16).at[slot_index].set(d_result)
    mixed_rows = (cells.astype(jnp.float32) + narrow(row_terms)).astype(jnp.bfloat16)
    outgoing = jnp.zeros((slot_total, feat_width), jnp.bfloat16).at[slot_index].set(mixed_rows)
    arrived, col_keys = (
        lax.all_to_all(outgoing, "band", split_axis=0, concat_axis=0, tiled=True),
        lax.all_to_all(keys_out, "band", split_axis=0, concat_axis=0, tiled=True),
    )
    column_full = widen(arrived)
    col_allowed = column_band_mask(col_keys)

    def col_local(inputs):
        return block_terms(inputs, col_gain, col_qkv, col_out, col_allowed, inputs.shape[0])

    col_terms, col_pull = jax.vjp(col_local, column_full)
    settled = (arrived.astype(jnp.float32) + narrow(col_terms)).astype(jnp.bfloat16)
    result = move_rows(settled)[slot_index]
    d_column = move_rows(back_in)
    (d_col_part,) = col_pull(widen(d_column).astype(jnp.float32))
    d_mixed_col = (d_column.astype(jnp.float32) + narrow(d_col_part.astype(jnp.float32))).astype(
        jnp.bfloat16
    )
    d_mixed = move_rows(d_mixed_col)[slot_index]
    (d_row_part,) = row_pull(widen(d_mixed).astype(jnp.float32))
    d_cells = (d_mixed.astype(jnp.float32) + narrow(d_row_part.astype(jnp.float32))).astype(
        jnp.bfloat16
    )
    return (result, d_cells)


def solution(mesh):
    in_specs = (
        P("band", "mp"),
        P(),
        P(None, None, "mp"),
        P("mp", None),
        P(),
        P(None, None, "mp"),
        P("mp", None),
        P("band"),
        P("band", None),
        P("band"),
        P("band", "mp"),
    )
    out_specs = (P("band", "mp"), P("band", "mp"))
    return jax.shard_map(
        on_device, mesh=mesh, in_specs=in_specs, out_specs=out_specs, check_vma=False
    )
```

profile of v0, /device:TPU:12, one launch (start us, length us, event | category | flops | bytes accessed | tf_op | source)
XLA Modules:
  0.0 185.7 jit_solution(5068009255196758206)
XLA Ops:
  7.2 7.5 %all_gather.12 = bf16[256,1024]{1,0:T(8,128)(2,1)S(1)} all-gather(bf16[256,256]{1,0:T(8,128)(2,1)} %param.11), channel_id=1, replica_groups=mesh['band'=8,'mp'=4] {'mp'}, dimensions={1}, use_global_device_ids=true | all-gather | bytes 655360 | tf_op jit(solution)/shard_map/all_gather | solution.py:46
  14.7 0.2 fusion.34
  14.9 2.1 %fusion.21 = bf16[3,256,256]{2,1,0:T(8,128)(2,1)S(1)} fusion(bf16[3,1024,256]{2,1,0:T(8,128)(2,1)} %param.13, bf16[256,1024]{1,0:T(8,128)(2,1)S(1)} %all_gather.12, f32[1024]{0:T(1024)} %param.12, f32[256]{0:T(256)S(1)} %fusion.63), kind=kOutput, calls=%fused_computation.50 | convolution fusion | flops 403898368 | bytes 2495488 | tf_op jit(solution)/shard_map/jvp(lu,xuh->xlh)/dot_general | solution.py:18
  17.0 0.2 reshape.325
  17.2 0.2 copy.58
  17.4 0.2 reshape.326
  17.6 0.2 copy.59
  17.8 0.2 reshape.324
  18.0 0.2 copy.60
  18.2 1.2 fusion.75
  19.4 1.3 fusion.29
  20.7 0.1 copy.62
  20.9 1.1 convolution_convert_fusion.3
  22.0 0.6 reduce-window.6
  22.6 0.2 slice_reduce_fusion
  23.0 2.2 %scatter_custom_fusion.1 = bf16[384]{0:T(512)(128)(2,1)S(1)} fusion(s32[256]{0:T(256)S(1)} %bitcast.165, bf16[256]{0:T(256)(128)(2,1)S(1)} %convert_element_type.209, bf16[]{:T(256)} %constant.12.clone.1), kind=kCustom, calls=%fused_computation.125 | custom fusion | bytes 770 | tf_op jit(solution)/shard_map/scatter | solution.py:91
  25.2 0.7 all_to_all.52
  25.8 6.2 %all-to-all-start.1 = ((bf16[8,48,1]{1,2,0:T(2,128)(2,1)}), bf16[8,48,1]{1,2,0:T(2,128)(2,1)S(1)}, u32[]{:S(2)}, u32[]{:S(2)}) async-start(bf16[8,48,1]{1,2,0:T(2,128)(2,1)} %all_to_all.52), calls=%async_computation.2 | async-start | bytes 8192 | tf_op jit(solution)/shard_map/all_to_all | solution.py:98
  32.1 2.5 %scatter_custom_fusion.2 = bf16[384,256]{1,0:T(8,128)(2,1)} fusion(s32[256]{0:T(256)S(1)} %bitcast.166, bf16[256,256]{1,0:T(8,128)(2,1)} %param.21, bf16[]{:T(256)} %constant.12.clone.1), kind=kCustom, calls=%fused_computation.103 | custom fusion | bytes 197120 | tf_op jit(solution)/shard_map/scatter | solution.py:93
  34.5 1.6 all-to-all-done.1
  36.2 5.7 %all-to-all-start.3 = ((bf16[8,48,256]{2,1,0:T(8,128)(2,1)}), bf16[8,48,256]{2,1,0:T(8,128)(2,1)S(1)}, u32[]{:S(2)}, u32[]{:S(2)}) async-start(bf16[8,48,256]{2,1,0:T(8,128)(2,1)} %bitcast.22), calls=%async_computation.5 | async-start | bytes 393216 | tf_op jit(solution)/shard_map/all_to_all | solution.py:56
  42.0 0.8 fusion.43
  42.8 1.8 reduce-scatter.5.cloned.1.call-done
  44.6 2.5 %scatter_custom_fusion = bf16[384,256]{1,0:T(8,128)(2,1)} fusion(s32[256]{0:T(256)S(1)} %bitcast.167, bf16[256,256]{1,0:T(8,128)(2,1)} %reduce-scatter.5.cloned.1.call-done, bf16[256,256]{1,0:T(8,128)(2,1)S(1)} %copy-done.12, bf16[]{:T(256)} %constant.12.clone.1), kind=kCustom, calls=%fused_computation.98 | custom fusion | flops 262144 | bytes 458754 | tf_op jit(solution)/shard_map/scatter | solution.py:95
  47.1 0.5 all-to-all-done.3
  47.5 5.7 %all-to-all-start = ((bf16[8,48,256]{2,1,0:T(8,128)(2,1)}), bf16[8,48,256]{2,1,0:T(8,128)(2,1)S(1)}, u32[]{:S(2)}, u32[]{:S(2)}) async-start(bf16[8,48,256]{2,1,0:T(8,128)(2,1)} %bitcast.10), calls=%async_computation.1 | async-start | bytes 393216 | tf_op jit(solution)/shard_map/all_to_all | solution.py:97
  53.2 7.9 %all_gather.14 = bf16[384,1024]{1,0:T(8,128)(2,1)S(1)} all-gather(bf16[384,256]{1,0:T(8,128)(2,1)S(1)} %bitcast.146), channel_id=1, replica_groups=mesh['band'=8,'mp'=4] {'mp'}, dimensions={1}, use_global_device_ids=true | all-gather | bytes 983040 | tf_op jit(solution)/shard_map/all_gather | solution.py:46
  61.2 0.5 convolution_convert_fusion.9
  61.6 8.9 %all_gather.13 = bf16[384,1024]{1,0:T(8,128)(2,1)S(1)} all-gather(bf16[384,256]{1,0:T(8,128)(2,1)S(1)} %bitcast.145), channel_id=1, replica_groups=mesh['band'=8,'mp'=4] {'mp'}, dimensions={1}, use_global_device_ids=true | all-gather | bytes 983040 | tf_op jit(solution)/shard_map/all_gather | solution.py:46
  70.5 0.2 fusion.10
  70.8 1.1 fusion.18
  71.9 0.8 fusion.73
  72.7 3.5 %fusion.76 = (f32[4,384]{1,0:T(4,128)S(1)}, f32[4,384,384]{1,2,0:T(8,128)}) fusion(pred[384,384]{0,1:T(8,128)(4,1)} %fusion.43, bf16[384,4,64]{0,2,1:T(8,128)(2,1)} %bitcast.159, bf16[384,4,64]{0,2,1:T(8,128)(2,1)} %bitcast.156), kind=kOutput, calls=%fused_computation.135 | convolution fusion | flops 77857152 | bytes 2906112 | tf_op jit(solution)/shard_map/jvp()/sub | solution.py:29
  76.3 3.7 %fusion.7 = (f32[4,384]{1,0:T(4,128)S(1)}, bf16[4,384,384]{1,2,0:T(8,128)(2,1)}, bf16[4,384,384]{1,2,0:T(8,128)(2,1)}) fusion(f32[4,384,384]{1,2,0:T(8,128)} %get-tuple-element.13, f32[4,384]{1,0:T(4,128)S(1)} %multiply_divide_fusion, f32[4,384]{1,0:T(4,128)S(1)} %get-tuple-element.12, bf16[4,64,384]{2,1,0:T(8,128)(2,1)S(1)} %bitcast.150, ...), kind=kOutput, calls=%fused_computation.19 | convolution fusion | flops 79624704 | bytes 5130240 | tf_op jit(solution)/shard_map/transpose(jvp(bhqk,bkhe->bqhe))/dot_general | solution.py:32
  80.0 3.9 %fusion.26 = bf16[1,1,384,4,64]{2,4,3,1,0:T(8,128)(2,1)} fusion(bf16[384,4,64]{0,2,1:T(8,128)(2,1)} %bitcast.160, bf16[4,384,384]{1,2,0:T(8,128)(2,1)} %get-tuple-element.14, f32[4,384]{1,0:T(4,128)S(1)} %neg.13, f32[4,384]{1,0:T(4,128)S(1)} %get-tuple-element.12, pred[384,384]{0,1:T(8,128)(4,1)} %fusion.43, bf16[384,4,64]{0,2,1:T(8,128)(2,1)S(1)} %bitcast.157), kind=kOutput, calls=%fused_computation.61 | convolution fusion | flops 156403584 | bytes 1929216 | tf_op jit(solution)/shard_map/transpose(jvp(bqhe,bkhe->bhqk))/dot_general | solution.py:25
  84.0 3.6 %fusion.27 = bf16[1,1,384,4,64]{2,4,3,1,0:T(8,128)(2,1)} fusion(bf16[384,4,64]{0,2,1:T(8,128)(2,1)S(1)} %bitcast.158, bf16[4,384,384]{1,2,0:T(8,128)(2,1)} %get-tuple-element.14, f32[4,384]{1,0:T(4,128)S(1)} %neg.13, f32[4,384]{1,0:T(4,128)S(1)} %get-tuple-element.12, pred[384,384]{0,1:T(8,128)(4,1)} %fusion.43, bf16[384,4,64]{0,2,1:T(8,128)(2,1)S(1)} %bitcast.161), kind=kOutput, calls=%fused_computation.62 | convolution fusion | flops 156403584 | bytes 1929216 | tf_op jit(solution)/shard_map/transpose(jvp(bqhe,bkhe->bhqk))/dot_general | solution.py:25
  87.6 1.8 fusion.28
  89.4 1.1 pad_add_fusion
  90.5 1.1 copy.69
  91.6 2.0 %fusion.13 = (f32[384]{0:T(512)S(1)}, bf16[384,1024]{1,0:T(8,128)(2,1)S(1)}) fusion(bf16[384,1024]{1,0:T(8,128)(2,1)S(1)} %all_gather.13, f32[1024]{0:T(1024)S(1)} %copy-done.20, bf16[3,1024,256]{2,1,0:T(8,128)(2,1)S(1)} %copy-done, bf16[3,384,256]{2,1,0:T(8,128)(2,1)} %copy.69), kind=kOutput, calls=%fused_computation.32 | convolution fusion | flops 606338688 | bytes 3741184 | tf_op jit(solution)/shard_map/transpose(jvp(lu,xuh->xlh))/dot_general | solution.py:18
  93.6 1.3 fusion.9
  94.9 24.0 %reduce-scatter.9.cloned.1.call-done = bf16[384,256]{1,0:T(8,128)(2,1)} async-done(((bf16[384,1024]{1,0:T(8,128)(2,1)}), bf16[384,256]{1,0:T(8,128)(2,1)}) %reduce-scatter.9.cloned.1.call-update) | async-done | bytes 196624 | tf_op jit(solution)/shard_map/reduce_scatter | solution.py:50
  118.9 1.7 add_convert_fusion
  120.7 6.0 %all-to-all-start.4 = ((bf16[8,48,256]{2,1,0:T(8,128)(2,1)}), bf16[8,48,256]{2,1,0:T(8,128)(2,1)S(1)}, u32[]{:S(2)}, u32[]{:S(2)}) async-start(bf16[8,48,256]{2,1,0:T(8,128)(2,1)} %bitcast.41), calls=%async_computation.7 | async-start | bytes 393216 | tf_op jit(solution)/shard_map/all_to_all | solution.py:56
  126.7 1.7 convolution_convert_fusion.10
  128.5 1.3 convolution_convert_fusion.1
  129.8 2.8 %all-to-all-done.4 = bf16[8,48,256]{2,1,0:T(8,128)(2,1)S(1)} async-done(((bf16[8,48,256]{2,1,0:T(8,128)(2,1)}), bf16[8,48,256]{2,1,0:T(8,128)(2,1)S(1)}, u32[]{:S(2)}, u32[]{:S(2)}) %all-to-all-start.4) | async-done | bytes 196640 | tf_op jit(solution)/shard_map/all_to_all | solution.py:56
  132.6 1.2 gather_fusion.1
  133.7 6.7 %all-gather = bf16[256,1024]{1,0:T(8,128)(2,1)S(1)} all-gather(bf16[256,256]{1,0:T(8,128)(2,1)S(1)} %gather_fusion.1), channel_id=2, replica_groups=mesh['band'=8,'mp'=4] {'mp'}, dimensions={1}, use_global_device_ids=true | all-gather | bytes 655360 | tf_op jit(solution)/shard_map/all_gather | solution.py:46
  140.5 0.3 convolution_convert_fusion.14
  141.0 1.3 multiply_reduce_fusion
  142.3 1.4 fusion.30
  143.7 0.2 fusion.32
  144.0 0.3 fusion.31
  144.3 0.4 copy.79
  144.8 0.3 reshape.278
  145.0 2.2 %fusion.37 = (f32[256]{0:T(256)S(1)}, f32[256,1024]{1,0:T(8,128)S(1)}) fusion(bf16[256,1024]{1,0:T(8,128)(2,1)S(1)} %all_gather.12, f32[1024]{0:T(1024)S(1)} %copy-done.21, bf16[3,1024,256]{2,1,0:T(8,128)(2,1)} %param.13, bf16[3,256,256]{1,2,0:T(8,128)(2,1)S(1)} %reshape.278), kind=kOutput, calls=%fused_computation.77 | convolution fusion | flops 404225792 | bytes 3544064 | tf_op jit(solution)/shard_map/transpose(jvp(lu,xuh->xlh))/dot_general | solution.py:18
  147.2 1.1 fusion.33
  148.3 5.0 %reduce-scatter.7.cloned.1.call-done = bf16[384,256]{1,0:T(8,128)(2,1)} async-done(((bf16[384,1024]{1,0:T(8,128)(2,1)}), bf16[384,256]{1,0:T(8,128)(2,1)}) %reduce-scatter.7.cloned.1.call-update) | async-done | bytes 196624 | tf_op jit(solution)/shard_map/reduce_scatter | solution.py:50
  153.3 1.0 add_convert_fusion.1
  154.3 11.7 %all_to_all.58 = bf16[8,48,256]{2,1,0:T(8,128)(2,1)S(1)} all-to-all(bf16[8,48,256]{2,1,0:T(8,128)(2,1)S(1)} %bitcast.149), channel_id=1, replica_groups=mesh['band'=8,'mp'=4] {'band'}, dimensions={0} | all-to-all | bytes 393216 | tf_op jit(solution)/shard_map/all_to_all | solution.py:56
  166.0 1.8 gather_fusion
  167.8 9.7 %reduce-scatter.11.cloned.1.call-done = bf16[256,256]{1,0:T(8,128)(2,1)} async-done(((bf16[256,1024]{1,0:T(8,128)(2,1)}), bf16[256,256]{1,0:T(8,128)(2,1)}) %reduce-scatter.11.cloned.1.call-update) | async-done | bytes 131088 | tf_op jit(solution)/shard_map/reduce_scatter | solution.py:50
  177.6 1.6 add_convert_fusion.2
  (80 shorter events, 0.9 us)
Async XLA Ops:
  7.2 63.6 %copy-start = (bf16[3,1024,256]{2,1,0:T(8,128)(2,1)S(1)}, bf16[3,1024,256]{2,1,0:T(8,128)(2,1)}, u32[]{:S(2)}) copy-start(bf16[3,1024,256]{2,1,0:T(8,128)(2,1)} %param.16) | copy-start | bytes 4718596
  7.2 37.4 %reduce-scatter.5.cloned.1.call-start = ((), (), s32[]{:S(2)}) async-start(), calls=%async_computation.9 | async-start | bytes 655360 | tf_op jit(solution)/shard_map/reduce_scatter | solution.py:50
  14.9 2.8 %copy-start.22 = (s32[256]{0:T(256)S(1)}, s32[256]{0:T(256)}, u32[]{:S(2)}) copy-start(s32[256]{0:T(256)} %param.18) | copy-start | bytes 3076
  17.4 2.0 %copy-start.15 = (bf16[2,128,4,64]{1,3,2,0:T(8,128)(2,1)}, bf16[2,128,4,64]{1,3,2,0:T(8,128)(2,1)S(1)}, u32[]{:S(2)}) copy-start(bf16[2,128,4,64]{1,3,2,0:T(8,128)(2,1)S(1)} %copy.58) | copy-start | bytes 393220
  17.5 3.3 %copy-start.3 = (bf16[256,1024]{1,0:T(8,128)(2,1)S(1)}, bf16[256,1024]{1,0:T(8,128)(2,1)}, u32[]{:S(2)}) copy-start(bf16[256,1024]{1,0:T(8,128)(2,1)} %param.14) | copy-start | bytes 1572868
  17.7 1.7 copy-start.17
  18.2 1.2 copy-start.9
  18.2 3.8 %copy-start.19 = (s32[256,1]{0,1:T(1,128)S(1)}, s32[256,1]{0,1:T(1,128)}, u32[]{:S(2)}) copy-start(s32[256,1]{0,1:T(1,128)} %param.19) | copy-start | bytes 3076
  18.2 4.7 %copy-start.23 = (s32[256]{0:T(256)S(1)}, s32[256]{0:T(256)}, u32[]{:S(2)}) copy-start(s32[256]{0:T(256)} %param.20) | copy-start | bytes 3076
  19.4 25.2 %copy-start.12 = (bf16[256,256]{1,0:T(8,128)(2,1)S(1)}, bf16[256,256]{1,0:T(8,128)(2,1)}, u32[]{:S(2)}) copy-start(bf16[256,256]{1,0:T(8,128)(2,1)} %param.11) | copy-start | bytes 393220
  20.7 40.4 %copy-start.1 = (bf16[256,1024]{1,0:T(8,128)(2,1)S(1)}, bf16[256,1024]{1,0:T(8,128)(2,1)}, u32[]{:S(2)}) copy-start(bf16[256,1024]{1,0:T(8,128)(2,1)} %param.17) | copy-start | bytes 1572868
  25.8 10.3 %all-to-all-start.1 = ((bf16[8,48,1]{1,2,0:T(2,128)(2,1)}), bf16[8,48,1]{1,2,0:T(2,128)(2,1)S(1)}, u32[]{:S(2)}, u32[]{:S(2)}) async-start(bf16[8,48,1]{1,2,0:T(2,128)(2,1)} %all_to_all.52), calls=%async_computation.2 | async-start | bytes 8192 | tf_op jit(solution)/shard_map/all_to_all | solution.py:98
  36.2 11.4 %all-to-all-start.3 = ((bf16[8,48,256]{2,1,0:T(8,128)(2,1)}), bf16[8,48,256]{2,1,0:T(8,128)(2,1)S(1)}, u32[]{:S(2)}, u32[]{:S(2)}) async-start(bf16[8,48,256]{2,1,0:T(8,128)(2,1)} %bitcast.22), calls=%async_computation.5 | async-start | bytes 393216 | tf_op jit(solution)/shard_map/all_to_all | solution.py:56
  47.1 23.7 %copy-start.20 = (f32[1024]{0:T(1024)S(1)}, f32[1024]{0:T(1024)}, u32[]{:S(2)}) copy-start(f32[1024]{0:T(1024)} %param.15) | copy-start | bytes 12292
  47.5 14.1 %copy-start.7 = (bf16[8,48,256]{2,1,0:T(8,128)(2,1)}, bf16[8,48,256]{2,1,0:T(8,128)(2,1)S(1)}, u32[]{:S(2)}) copy-start(bf16[8,48,256]{2,1,0:T(8,128)(2,1)S(1)} %all-to-all-done.3) | copy-start | bytes 589828
  47.5 14.1 %all-to-all-start = ((bf16[8,48,256]{2,1,0:T(8,128)(2,1)}), bf16[8,48,256]{2,1,0:T(8,128)(2,1)S(1)}, u32[]{:S(2)}, u32[]{:S(2)}) async-start(bf16[8,48,256]{2,1,0:T(8,128)(2,1)} %bitcast.10), calls=%async_computation.1 | async-start | bytes 393216 | tf_op jit(solution)/shard_map/all_to_all | solution.py:97
  53.2 65.7 %reduce-scatter.9.cloned.1.call-start = ((), (), s32[]{:S(2)}) async-start(), calls=%async_computation.11 | async-start | bytes 983040 | tf_op jit(solution)/shard_map/reduce_scatter | solution.py:50
  61.6 10.3 %copy-start.5 = (bf16[8,48,256]{2,1,0:T(8,128)(2,1)}, bf16[8,48,256]{2,1,0:T(8,128)(2,1)S(1)}, u32[]{:S(2)}) copy-start(bf16[8,48,256]{2,1,0:T(8,128)(2,1)S(1)} %all-to-all-done) | copy-start | bytes 589828
  72.7 7.3 %copy-start.8 = (bf16[1,384,256]{1,2,0:T(8,128)(2,1)}, bf16[1,384,256]{1,2,0:T(8,128)(2,1)S(1)}, u32[]{:S(2)}) copy-start(bf16[1,384,256]{1,2,0:T(8,128)(2,1)S(1)} %get-tuple-element.6) | copy-start | bytes 589828
  76.3 3.7 %copy-start.13 = (bf16[1,384,256]{1,2,0:T(8,128)(2,1)S(1)}, bf16[1,384,256]{1,2,0:T(8,128)(2,1)}, u32[]{:S(2)}) copy-start(bf16[1,384,256]{1,2,0:T(8,128)(2,1)} %get-tuple-element.4) | copy-start | bytes 589828
  80.0 3.9 %copy-start.14 = (bf16[1,384,256]{1,2,0:T(8,128)(2,1)S(1)}, bf16[1,384,256]{1,2,0:T(8,128)(2,1)}, u32[]{:S(2)}) copy-start(bf16[1,384,256]{1,2,0:T(8,128)(2,1)} %get-tuple-element.5) | copy-start | bytes 589828
  93.6 34.9 %copy-start.2 = (bf16[256,1024]{1,0:T(8,128)(2,1)S(1)}, bf16[256,1024]{1,0:T(8,128)(2,1)}, u32[]{:S(2)}) copy-start(bf16[256,1024]{1,0:T(8,128)(2,1)} %param.17) | copy-start | bytes 1572868
  120.7 11.9 %all-to-all-start.4 = ((bf16[8,48,256]{2,1,0:T(8,128)(2,1)}), bf16[8,48,256]{2,1,0:T(8,128)(2,1)S(1)}, u32[]{:S(2)}, u32[]{:S(2)}) async-start(bf16[8,48,256]{2,1,0:T(8,128)(2,1)} %bitcast.41), calls=%async_computation.7 | async-start | bytes 393216 | tf_op jit(solution)/shard_map/all_to_all | solution.py:56
  126.7 26.6 %reduce-scatter.7.cloned.1.call-start = ((), (), s32[]{:S(2)}) async-start(), calls=%async_computation.10 | async-start | bytes 983040 | tf_op jit(solution)/shard_map/reduce_scatter | solution.py:50
  128.4 12.0 %copy-start.4 = (bf16[256,1024]{1,0:T(8,128)(2,1)S(1)}, bf16[256,1024]{1,0:T(8,128)(2,1)}, u32[]{:S(2)}) copy-start(bf16[256,1024]{1,0:T(8,128)(2,1)} %param.14) | copy-start | bytes 1572868
  129.7 11.2 %copy-start.10 = (bf16[2,128,4,64]{1,3,2,0:T(8,128)(2,1)S(1)}, bf16[2,128,4,64]{1,3,2,0:T(8,128)(2,1)}, u32[]{:S(2)}) copy-start(bf16[2,128,4,64]{1,3,2,0:T(8,128)(2,1)} %copy-done.9) | copy-start | bytes 393220
  129.8 47.8 %reduce-scatter.11.cloned.1.call-start = ((), (), s32[]{:S(2)}) async-start(), calls=%async_computation.12 | async-start | bytes 655360 | tf_op jit(solution)/shard_map/reduce_scatter | solution.py:50
  140.5 3.2 %copy-start.18 = (bf16[2,128,4,64]{1,3,2,0:T(8,128)(2,1)S(1)}, bf16[2,128,4,64]{1,3,2,0:T(8,128)(2,1)}, u32[]{:S(2)}) copy-start(bf16[2,128,4,64]{1,3,2,0:T(8,128)(2,1)} %copy-done.17) | copy-start | bytes 393220
  140.8 2.9 %copy-start.11 = (f32[2,4,128,128]{2,3,1,0:T(8,128)S(1)}, f32[2,4,128,128]{2,3,1,0:T(8,128)}, u32[]{:S(2)}) copy-start(f32[2,4,128,128]{2,3,1,0:T(8,128)} %get-tuple-element.11) | copy-start | bytes 1572868
  142.3 1.7 copy-start.16
  144.0 1.0 copy-start.21
  145.0 8.3 %copy-start.6 = (bf16[8,48,256]{2,1,0:T(8,128)(2,1)S(1)}, bf16[8,48,256]{2,1,0:T(8,128)(2,1)}, u32[]{:S(2)}) copy-start(bf16[8,48,256]{2,1,0:T(8,128)(2,1)} %copy-done.5) | copy-start | bytes 589828
Sparse Core Ops, SparseCore 0:
  22.1 22.3 reduce-scatter.4
  95.0 23.8 reduce-scatter.8
  130.1 23.2 reduce-scatter.6
  155.8 21.6 reduce-scatter.10
where the time goes:
time: 188 us; the launch traced here: 186 us
  waiting for transfers between devices  45.5 us (24%)
  blocking collectives  42.7 us (23%)
  matrix products  34.5 us (18%)
  starting transfers between devices  23.7 us (13%)
  between operations  14.2 us (8%)
  local copies, waits for them, and re-layouts  12.5 us (7%)
  other arithmetic  12.5 us (7%)
    reduce_scatter x4, waiting for transfers between devices, narrow(): lax.psum_scatter(terms.astype(jnp.bfloat16), 'mp', scatter_dimension=1, t...  40.6 us
    all_gather x4, blocking collectives, widen(): return lax.all_gather(block, 'mp', axis=1, tiled=True)  31 us
    all_to_all x2, starting transfers between devices, move_rows(): return lax.all_to_all(rows, 'band', split_axis=0, concat_axis=0, tiled=True)  11.7 us
    all_to_all x1, blocking collectives, move_rows(): return lax.all_to_all(rows, 'band', split_axis=0, concat_axis=0, tiled=True)  11.7 us
    dot_general x6, matrix products, block_terms(): jnp.einsum('bhqk,bkhe->bqhe', attn_probs, shaped[2], preferred_element_ty...  11.2 us
    dot_general x4, matrix products, block_terms(): jnp.einsum('bqhe,bkhe->bhqk', shaped[0], shaped[1], preferred_element_typ...  8.12 us
    dot_general x4, matrix products, block_terms(): jnp.einsum('lu,xuh->xlh', normalized_cells, query_key_value_weight, prefe...  7.3 us
    all_to_all x1, starting transfers between devices, on_device(): lax.all_to_all(keys_out, 'band', split_axis=0, concat_axis=0, tiled=True)  6.22 us
  transfers between devices with their start and end apart: 8, of which 7 were waited for; matrix products, arithmetic and copies ran while one was open for 13% of the time, Pallas kernels for 0%

commit v1 on v0

--- a/solution.py
+++ b/solution.py
@@ -82,8 +82,9 @@
 
     row_terms, row_pull = jax.vjp(row_local, gathered)
     target = col_dest[:, 0]
-    onehot = (target[:, None] == jnp.arange(band_count, dtype=jnp.int32)[None, :]).astype(jnp.int32)
-    ranking = jnp.sum((jnp.cumsum(onehot, axis=0) - onehot) * onehot, axis=1)
+    place = jnp.arange(cell_rows, dtype=jnp.int32)
+    earlier = (target[:, None] == target[None, :]) & (place[None, :] < place[:, None])
+    ranking = jnp.sum(earlier.astype(jnp.int32), axis=1)
     slot_index = target * capacity + ranking
     keys_out = (
         jnp.zeros((slot_total,), jnp.bfloat16)

time: 188 us -> 188 us (level)
  transfers between devices with their start and end apart: 8 -> 8, of which waited for: 7 -> 6; matrix products, arithmetic and copies ran while one was open for 13% -> 13% of each run, Pallas kernels for 0% -> 0%
where the time goes in v1:
time: 188 us; the launch traced here: 186 us
  waiting for transfers between devices  46 us (24%)
  blocking collectives  42.5 us (23%)
  matrix products  34.5 us (18%)
  starting transfers between devices  24.2 us (13%)
  between operations  14.2 us (8%)
  local copies, waits for them, and re-layouts  12.3 us (7%)
  other arithmetic  11.9 us (6%)
    reduce_scatter x4, waiting for transfers between devices, narrow(): lax.psum_scatter(terms.astype(jnp.bfloat16), 'mp', scatter_dimension=1, t...  41.6 us
    all_gather x4, blocking collectives, widen(): return lax.all_gather(block, 'mp', axis=1, tiled=True)  30.8 us
    all_to_all x2, starting transfers between devices, move_rows(): return lax.all_to_all(rows, 'band', split_axis=0, concat_axis=0, tiled=True)  11.7 us
    all_to_all x1, blocking collectives, move_rows(): return lax.all_to_all(rows, 'band', split_axis=0, concat_axis=0, tiled=True)  11.7 us
    dot_general x6, matrix products, block_terms(): jnp.einsum('bhqk,bkhe->bqhe', attn_probs, shaped[2], preferred_element_ty...  11.2 us
    dot_general x4, matrix products, block_terms(): jnp.einsum('bqhe,bkhe->bhqk', shaped[0], shaped[1], preferred_element_typ...  8.12 us
    dot_general x4, matrix products, block_terms(): jnp.einsum('lu,xuh->xlh', normalized_cells, query_key_value_weight, prefe...  7.29 us
    all_to_all x1, starting transfers between devices, on_device(): lax.all_to_all(keys_out, 'band', split_axis=0, concat_axis=0, tiled=True)  6.23 us
  transfers between devices with their start and end apart: 8, of which 6 were waited for; matrix products, arithmetic and copies ran while one was open for 13% of the time, Pallas kernels for 0%

profile of v1, /device:TPU:12, one launch (start us, length us, event | category | flops | bytes accessed | tf_op | source)
XLA Modules:
  0.0 185.7 jit_solution(12250987462010092255)
XLA Ops:
  7.2 7.5 %all_gather.12 = bf16[256,1024]{1,0:T(8,128)(2,1)S(1)} all-gather(bf16[256,256]{1,0:T(8,128)(2,1)} %param.11), channel_id=1, replica_groups=mesh['band'=8,'mp'=4] {'mp'}, dimensions={1}, use_global_device_ids=true | all-gather | bytes 655360 | tf_op jit(solution)/shard_map/all_gather | solution.py:46
  14.7 0.2 fusion.34
  14.9 2.1 %fusion.21 = bf16[3,256,256]{2,1,0:T(8,128)(2,1)S(1)} fusion(bf16[3,1024,256]{2,1,0:T(8,128)(2,1)} %param.13, bf16[256,1024]{1,0:T(8,128)(2,1)S(1)} %all_gather.12, f32[1024]{0:T(1024)} %param.12, f32[256]{0:T(256)S(1)} %fusion.61), kind=kOutput, calls=%fused_computation.50 | convolution fusion | flops 403898368 | bytes 2495488 | tf_op jit(solution)/shard_map/jvp(lu,xuh->xlh)/dot_general | solution.py:18
  17.0 0.2 reshape.309
  17.2 0.2 copy.84
  17.4 0.2 reshape.310
  17.6 0.2 copy.85
  17.7 0.1 broadcast_compare_fusion
  17.8 0.2 reshape.308
  18.0 0.2 copy.86
  18.2 1.2 fusion.73
  19.4 1.3 fusion.29
  20.7 0.1 copy.88
  20.9 1.1 convolution_convert_fusion.3
  22.0 0.2 convert_reduce_fusion
  22.2 2.2 %scatter_custom_fusion.1 = bf16[384]{0:T(512)(128)(2,1)S(1)} fusion(s32[256]{0:T(256)S(1)} %bitcast.155, bf16[256]{0:T(256)(128)(2,1)S(1)} %convert_element_type.204, bf16[]{:T(256)} %constant.12.clone.1), kind=kCustom, calls=%fused_computation.121 | custom fusion | bytes 770 | tf_op jit(solution)/shard_map/scatter | solution.py:92
  24.4 0.7 all_to_all.52
  25.1 6.2 %all-to-all-start.1 = ((bf16[8,48,1]{1,2,0:T(2,128)(2,1)}), bf16[8,48,1]{1,2,0:T(2,128)(2,1)S(1)}, u32[]{:S(2)}, u32[]{:S(2)}) async-start(bf16[8,48,1]{1,2,0:T(2,128)(2,1)} %all_to_all.52), calls=%async_computation.2 | async-start | bytes 8192 | tf_op jit(solution)/shard_map/all_to_all | solution.py:99
  31.3 2.5 %scatter_custom_fusion.2 = bf16[384,256]{1,0:T(8,128)(2,1)} fusion(s32[256]{0:T(256)S(1)} %bitcast.156, bf16[256,256]{1,0:T(8,128)(2,1)} %param.21, bf16[]{:T(256)} %constant.12.clone.1), kind=kCustom, calls=%fused_computation.106 | custom fusion | bytes 197120 | tf_op jit(solution)/shard_map/scatter | solution.py:94
  33.8 1.6 all-to-all-done.1
  35.4 5.7 %all-to-all-start.3 = ((bf16[8,48,256]{2,1,0:T(8,128)(2,1)}), bf16[8,48,256]{2,1,0:T(8,128)(2,1)S(1)}, u32[]{:S(2)}, u32[]{:S(2)}) async-start(bf16[8,48,256]{2,1,0:T(8,128)(2,1)} %bitcast.19), calls=%async_computation.5 | async-start | bytes 393216 | tf_op jit(solution)/shard_map/all_to_all | solution.py:56
  41.2 0.8 fusion.43
  42.1 2.5 %reduce-scatter.5.cloned.1.call-done = bf16[256,256]{1,0:T(8,128)(2,1)} async-done(((bf16[256,1024]{1,0:T(8,128)(2,1)}), bf16[256,256]{1,0:T(8,128)(2,1)}) %reduce-scatter.5.cloned.1.call-update) | async-done | bytes 131088 | tf_op jit(solution)/shard_map/reduce_scatter | solution.py:50
  44.5 2.5 %scatter_custom_fusion = bf16[384,256]{1,0:T(8,128)(2,1)} fusion(s32[256]{0:T(256)S(1)} %bitcast.157, bf16[256,256]{1,0:T(8,128)(2,1)} %reduce-scatter.5.cloned.1.call-done, bf16[256,256]{1,0:T(8,128)(2,1)S(1)} %copy-done.12, bf16[]{:T(256)} %constant.12.clone.1), kind=kCustom, calls=%fused_computation.101 | custom fusion | flops 262144 | bytes 458754 | tf_op jit(solution)/shard_map/scatter | solution.py:96
  47.0 6.2 %all-to-all-start = ((bf16[8,48,256]{2,1,0:T(8,128)(2,1)}), bf16[8,48,256]{2,1,0:T(8,128)(2,1)S(1)}, u32[]{:S(2)}, u32[]{:S(2)}) async-start(bf16[8,48,256]{2,1,0:T(8,128)(2,1)} %bitcast.7), calls=%async_computation.1 | async-start | bytes 393216 | tf_op jit(solution)/shard_map/all_to_all | solution.py:98
  53.2 7.6 %all_gather.14 = bf16[384,1024]{1,0:T(8,128)(2,1)S(1)} all-gather(bf16[384,256]{1,0:T(8,128)(2,1)S(1)} %bitcast.137), channel_id=1, replica_groups=mesh['band'=8,'mp'=4] {'mp'}, dimensions={1}, use_global_device_ids=true | all-gather | bytes 983040 | tf_op jit(solution)/shard_map/all_gather | solution.py:46
  60.9 0.5 convolution_convert_fusion.9
  61.3 8.9 %all_gather.13 = bf16[384,1024]{1,0:T(8,128)(2,1)S(1)} all-gather(bf16[384,256]{1,0:T(8,128)(2,1)S(1)} %bitcast.136), channel_id=1, replica_groups=mesh['band'=8,'mp'=4] {'mp'}, dimensions={1}, use_global_device_ids=true | all-gather | bytes 983040 | tf_op jit(solution)/shard_map/all_gather | solution.py:46
  70.2 0.2 fusion.10
  70.5 1.1 fusion.18
  71.6 0.8 fusion.71
  72.4 3.5 %fusion.74 = (f32[4,384]{1,0:T(4,128)S(1)}, f32[4,384,384]{1,2,0:T(8,128)}) fusion(pred[384,384]{0,1:T(8,128)(4,1)} %fusion.43, bf16[384,4,64]{0,2,1:T(8,128)(2,1)} %bitcast.150, bf16[384,4,64]{0,2,1:T(8,128)(2,1)} %bitcast.147), kind=kOutput, calls=%fused_computation.131 | convolution fusion | flops 77857152 | bytes 2906112 | tf_op jit(solution)/shard_map/jvp()/sub | solution.py:29
  76.0 3.7 %fusion.7 = (f32[4,384]{1,0:T(4,128)S(1)}, bf16[4,384,384]{1,2,0:T(8,128)(2,1)}, bf16[4,384,384]{1,2,0:T(8,128)(2,1)}) fusion(f32[4,384,384]{1,2,0:T(8,128)} %get-tuple-element.13, f32[4,384]{1,0:T(4,128)S(1)} %multiply_divide_fusion, f32[4,384]{1,0:T(4,128)S(1)} %get-tuple-element.12, bf16[4,64,384]{2,1,0:T(8,128)(2,1)S(1)} %bitcast.141, ...), kind=kOutput, calls=%fused_computation.19 | convolution fusion | flops 79624704 | bytes 5130240 | tf_op jit(solution)/shard_map/transpose(jvp(bhqk,bkhe->bqhe))/dot_general | solution.py:32
  79.7 3.9 %fusion.26 = bf16[1,1,384,4,64]{2,4,3,1,0:T(8,128)(2,1)} fusion(bf16[384,4,64]{0,2,1:T(8,128)(2,1)} %bitcast.151, bf16[4,384,384]{1,2,0:T(8,128)(2,1)} %get-tuple-element.14, f32[4,384]{1,0:T(4,128)S(1)} %neg.13, f32[4,384]{1,0:T(4,128)S(1)} %get-tuple-element.12, pred[384,384]{0,1:T(8,128)(4,1)} %fusion.43, bf16[384,4,64]{0,2,1:T(8,128)(2,1)S(1)} %bitcast.148), kind=kOutput, calls=%fused_computation.61 | convolution fusion | flops 156403584 | bytes 1929216 | tf_op jit(solution)/shard_map/transpose(jvp(bqhe,bkhe->bhqk))/dot_general | solution.py:25
  83.7 3.6 %fusion.27 = bf16[1,1,384,4,64]{2,4,3,1,0:T(8,128)(2,1)} fusion(bf16[384,4,64]{0,2,1:T(8,128)(2,1)S(1)} %bitcast.149, bf16[4,384,384]{1,2,0:T(8,128)(2,1)} %get-tuple-element.14, f32[4,384]{1,0:T(4,128)S(1)} %neg.13, f32[4,384]{1,0:T(4,128)S(1)} %get-tuple-element.12, pred[384,384]{0,1:T(8,128)(4,1)} %fusion.43, bf16[384,4,64]{0,2,1:T(8,128)(2,1)S(1)} %bitcast.152), kind=kOutput, calls=%fused_computation.62 | convolution fusion | flops 156403584 | bytes 1929216 | tf_op jit(solution)/shard_map/transpose(jvp(bqhe,bkhe->bhqk))/dot_general | solution.py:25
  87.3 1.8 fusion.28
  89.1 1.1 pad_add_fusion
  90.2 1.1 copy.95
  91.3 2.0 %fusion.13 = (f32[384]{0:T(512)S(1)}, bf16[384,1024]{1,0:T(8,128)(2,1)S(1)}) fusion(bf16[384,1024]{1,0:T(8,128)(2,1)S(1)} %all_gather.13, f32[1024]{0:T(1024)S(1)} %copy-done.20, bf16[3,1024,256]{2,1,0:T(8,128)(2,1)S(1)} %copy-done, bf16[3,384,256]{2,1,0:T(8,128)(2,1)} %copy.95), kind=kOutput, calls=%fused_computation.32 | convolution fusion | flops 606338688 | bytes 3741184 | tf_op jit(solution)/shard_map/transpose(jvp(lu,xuh->xlh))/dot_general | solution.py:18
  93.3 1.3 fusion.9
  94.6 24.3 %reduce-scatter.9.cloned.1.call-done = bf16[384,256]{1,0:T(8,128)(2,1)} async-done(((bf16[384,1024]{1,0:T(8,128)(2,1)}), bf16[384,256]{1,0:T(8,128)(2,1)}) %reduce-scatter.9.cloned.1.call-update) | async-done | bytes 196624 | tf_op jit(solution)/shard_map/reduce_scatter | solution.py:50
  118.9 1.7 add_convert_fusion
  120.7 6.1 %all-to-all-start.4 = ((bf16[8,48,256]{2,1,0:T(8,128)(2,1)}), bf16[8,48,256]{2,1,0:T(8,128)(2,1)S(1)}, u32[]{:S(2)}, u32[]{:S(2)}) async-start(bf16[8,48,256]{2,1,0:T(8,128)(2,1)} %bitcast.38), calls=%async_computation.7 | async-start | bytes 393216 | tf_op jit(solution)/shard_map/all_to_all | solution.py:56
  126.7 1.7 convolution_convert_fusion.10
  128.4 1.3 convolution_convert_fusion.1
  129.8 2.8 %all-to-all-done.4 = bf16[8,48,256]{2,1,0:T(8,128)(2,1)S(1)} async-done(((bf16[8,48,256]{2,1,0:T(8,128)(2,1)}), bf16[8,48,256]{2,1,0:T(8,128)(2,1)S(1)}, u32[]{:S(2)}, u32[]{:S(2)}) %all-to-all-start.4) | async-done | bytes 196640 | tf_op jit(solution)/shard_map/all_to_all | solution.py:56
  132.6 1.2 gather_fusion.1
  133.7 6.7 %all-gather = bf16[256,1024]{1,0:T(8,128)(2,1)S(1)} all-gather(bf16[256,256]{1,0:T(8,128)(2,1)S(1)} %gather_fusion.1), channel_id=2, replica_groups=mesh['band'=8,'mp'=4] {'mp'}, dimensions={1}, use_global_device_ids=true | all-gather | bytes 655360 | tf_op jit(solution)/shard_map/all_gather | solution.py:46
  140.4 0.3 convolution_convert_fusion.14
  140.8 0.1 copy.96
  140.9 1.3 multiply_reduce_fusion
  142.3 1.4 fusion.30
  143.7 0.2 fusion.32
  144.0 0.3 fusion.31
  144.3 0.4 copy.105
  144.7 0.3 reshape.262
  145.0 2.2 %fusion.37 = (f32[256]{0:T(256)S(1)}, f32[256,1024]{1,0:T(8,128)S(1)}) fusion(bf16[256,1024]{1,0:T(8,128)(2,1)S(1)} %all_gather.12, f32[1024]{0:T(1024)S(1)} %copy-done.21, bf16[3,1024,256]{2,1,0:T(8,128)(2,1)} %param.13, bf16[3,256,256]{1,2,0:T(8,128)(2,1)S(1)} %reshape.262), kind=kOutput, calls=%fused_computation.77 | convolution fusion | flops 404225792 | bytes 3544064 | tf_op jit(solution)/shard_map/transpose(jvp(lu,xuh->xlh))/dot_general | solution.py:18
  147.2 1.1 fusion.33
  148.3 5.0 %reduce-scatter.7.cloned.1.call-done = bf16[384,256]{1,0:T(8,128)(2,1)} async-done(((bf16[384,1024]{1,0:T(8,128)(2,1)}), bf16[384,256]{1,0:T(8,128)(2,1)}) %reduce-scatter.7.cloned.1.call-update) | async-done | bytes 196624 | tf_op jit(solution)/shard_map/reduce_scatter | solution.py:50
  153.3 1.0 add_convert_fusion.1
  154.3 11.7 %all_to_all.58 = bf16[8,48,256]{2,1,0:T(8,128)(2,1)S(1)} all-to-all(bf16[8,48,256]{2,1,0:T(8,128)(2,1)S(1)} %bitcast.140), channel_id=1, replica_groups=mesh['band'=8,'mp'=4] {'band'}, dimensions={0} | all-to-all | bytes 393216 | tf_op jit(solution)/shard_map/all_to_all | solution.py:56
  166.0 1.8 gather_fusion
  167.8 9.7 %reduce-scatter.11.cloned.1.call-done = bf16[256,256]{1,0:T(8,128)(2,1)} async-done(((bf16[256,1024]{1,0:T(8,128)(2,1)}), bf16[256,256]{1,0:T(8,128)(2,1)}) %reduce-scatter.11.cloned.1.call-update) | async-done | bytes 131088 | tf_op jit(solution)/shard_map/reduce_scatter | solution.py:50
  177.5 1.6 add_convert_fusion.2
  (75 shorter events, 0.6 us)
Async XLA Ops:
  7.2 63.3 %copy-start = (bf16[3,1024,256]{2,1,0:T(8,128)(2,1)S(1)}, bf16[3,1024,256]{2,1,0:T(8,128)(2,1)}, u32[]{:S(2)}) copy-start(bf16[3,1024,256]{2,1,0:T(8,128)(2,1)} %param.16) | copy-start | bytes 4718596
  7.2 37.4 %reduce-scatter.5.cloned.1.call-start = ((), (), s32[]{:S(2)}) async-start(), calls=%async_computation.9 | async-start | bytes 655360 | tf_op jit(solution)/shard_map/reduce_scatter | solution.py:50
  14.9 2.8 %copy-start.22 = (s32[256]{0:T(256)S(1)}, s32[256]{0:T(256)}, u32[]{:S(2)}) copy-start(s32[256]{0:T(256)} %param.18) | copy-start | bytes 3076
  17.4 0.8 copy-start.15
  17.5 3.3 %copy-start.3 = (bf16[256,1024]{1,0:T(8,128)(2,1)S(1)}, bf16[256,1024]{1,0:T(8,128)(2,1)}, u32[]{:S(2)}) copy-start(bf16[256,1024]{1,0:T(8,128)(2,1)} %param.14) | copy-start | bytes 1572868
  17.7 1.7 copy-start.17
  18.2 1.2 copy-start.9
  18.2 3.8 %copy-start.23 = (s32[256]{0:T(256)S(1)}, s32[256]{0:T(256)}, u32[]{:S(2)}) copy-start(s32[256]{0:T(256)} %param.20) | copy-start | bytes 3076
  18.2 3.8 %copy-start.19 = (s32[256,1]{0,1:T(1,128)S(1)}, s32[256,1]{0,1:T(1,128)}, u32[]{:S(2)}) copy-start(s32[256,1]{0,1:T(1,128)} %param.19) | copy-start | bytes 3076
  19.4 25.1 %copy-start.12 = (bf16[256,256]{1,0:T(8,128)(2,1)S(1)}, bf16[256,256]{1,0:T(8,128)(2,1)}, u32[]{:S(2)}) copy-start(bf16[256,256]{1,0:T(8,128)(2,1)} %param.11) | copy-start | bytes 393220
  20.7 40.1 %copy-start.1 = (bf16[256,1024]{1,0:T(8,128)(2,1)S(1)}, bf16[256,1024]{1,0:T(8,128)(2,1)}, u32[]{:S(2)}) copy-start(bf16[256,1024]{1,0:T(8,128)(2,1)} %param.17) | copy-start | bytes 1572868
  25.1 10.3 %all-to-all-start.1 = ((bf16[8,48,1]{1,2,0:T(2,128)(2,1)}), bf16[8,48,1]{1,2,0:T(2,128)(2,1)S(1)}, u32[]{:S(2)}, u32[]{:S(2)}) async-start(bf16[8,48,1]{1,2,0:T(2,128)(2,1)} %all_to_all.52), calls=%async_computation.2 | async-start | bytes 8192 | tf_op jit(solution)/shard_map/all_to_all | solution.py:99
  35.4 11.6 %all-to-all-start.3 = ((bf16[8,48,256]{2,1,0:T(8,128)(2,1)}), bf16[8,48,256]{2,1,0:T(8,128)(2,1)S(1)}, u32[]{:S(2)}, u32[]{:S(2)}) async-start(bf16[8,48,256]{2,1,0:T(8,128)(2,1)} %bitcast.19), calls=%async_computation.5 | async-start | bytes 393216 | tf_op jit(solution)/shard_map/all_to_all | solution.py:56
  47.0 23.5 %copy-start.20 = (f32[1024]{0:T(1024)S(1)}, f32[1024]{0:T(1024)}, u32[]{:S(2)}) copy-start(f32[1024]{0:T(1024)} %param.15) | copy-start | bytes 12292
  47.0 14.3 %copy-start.7 = (bf16[8,48,256]{2,1,0:T(8,128)(2,1)}, bf16[8,48,256]{2,1,0:T(8,128)(2,1)S(1)}, u32[]{:S(2)}) copy-start(bf16[8,48,256]{2,1,0:T(8,128)(2,1)S(1)} %all-to-all-done.3) | copy-start | bytes 589828
  47.0 14.3 %all-to-all-start = ((bf16[8,48,256]{2,1,0:T(8,128)(2,1)}), bf16[8,48,256]{2,1,0:T(8,128)(2,1)S(1)}, u32[]{:S(2)}, u32[]{:S(2)}) async-start(bf16[8,48,256]{2,1,0:T(8,128)(2,1)} %bitcast.7), calls=%async_computation.1 | async-start | bytes 393216 | tf_op jit(solution)/shard_map/all_to_all | solution.py:98
  53.2 65.7 %reduce-scatter.9.cloned.1.call-start = ((), (), s32[]{:S(2)}) async-start(), calls=%async_computation.11 | async-start | bytes 983040 | tf_op jit(solution)/shard_map/reduce_scatter | solution.py:50
  61.3 10.3 %copy-start.5 = (bf16[8,48,256]{2,1,0:T(8,128)(2,1)}, bf16[8,48,256]{2,1,0:T(8,128)(2,1)S(1)}, u32[]{:S(2)}) copy-start(bf16[8,48,256]{2,1,0:T(8,128)(2,1)S(1)} %all-to-all-done) | copy-start | bytes 589828
  72.4 7.3 %copy-start.8 = (bf16[1,384,256]{1,2,0:T(8,128)(2,1)}, bf16[1,384,256]{1,2,0:T(8,128)(2,1)S(1)}, u32[]{:S(2)}) copy-start(bf16[1,384,256]{1,2,0:T(8,128)(2,1)S(1)} %get-tuple-element.6) | copy-start | bytes 589828
  76.0 3.7 %copy-start.13 = (bf16[1,384,256]{1,2,0:T(8,128)(2,1)S(1)}, bf16[1,384,256]{1,2,0:T(8,128)(2,1)}, u32[]{:S(2)}) copy-start(bf16[1,384,256]{1,2,0:T(8,128)(2,1)} %get-tuple-element.4) | copy-start | bytes 589828
  79.7 3.9 %copy-start.14 = (bf16[1,384,256]{1,2,0:T(8,128)(2,1)S(1)}, bf16[1,384,256]{1,2,0:T(8,128)(2,1)}, u32[]{:S(2)}) copy-start(bf16[1,384,256]{1,2,0:T(8,128)(2,1)} %get-tuple-element.5) | copy-start | bytes 589828
  93.3 35.2 %copy-start.2 = (bf16[256,1024]{1,0:T(8,128)(2,1)S(1)}, bf16[256,1024]{1,0:T(8,128)(2,1)}, u32[]{:S(2)}) copy-start(bf16[256,1024]{1,0:T(8,128)(2,1)} %param.17) | copy-start | bytes 1572868
  120.7 11.9 %all-to-all-start.4 = ((bf16[8,48,256]{2,1,0:T(8,128)(2,1)}), bf16[8,48,256]{2,1,0:T(8,128)(2,1)S(1)}, u32[]{:S(2)}, u32[]{:S(2)}) async-start(bf16[8,48,256]{2,1,0:T(8,128)(2,1)} %bitcast.38), calls=%async_computation.7 | async-start | bytes 393216 | tf_op jit(solution)/shard_map/all_to_all | solution.py:56
  126.7 26.6 %reduce-scatter.7.cloned.1.call-start = ((), (), s32[]{:S(2)}) async-start(), calls=%async_computation.10 | async-start | bytes 983040 | tf_op jit(solution)/shard_map/reduce_scatter | solution.py:50
  128.4 12.0 %copy-start.4 = (bf16[256,1024]{1,0:T(8,128)(2,1)S(1)}, bf16[256,1024]{1,0:T(8,128)(2,1)}, u32[]{:S(2)}) copy-start(bf16[256,1024]{1,0:T(8,128)(2,1)} %param.14) | copy-start | bytes 1572868
  129.7 11.2 %copy-start.10 = (bf16[2,128,4,64]{1,3,2,0:T(8,128)(2,1)S(1)}, bf16[2,128,4,64]{1,3,2,0:T(8,128)(2,1)}, u32[]{:S(2)}) copy-start(bf16[2,128,4,64]{1,3,2,0:T(8,128)(2,1)} %copy-done.9) | copy-start | bytes 393220
  129.7 47.8 %reduce-scatter.11.cloned.1.call-start = ((), (), s32[]{:S(2)}) async-start(), calls=%async_computation.12 | async-start | bytes 655360 | tf_op jit(solution)/shard_map/reduce_scatter | solution.py:50
  140.4 3.2 %copy-start.18 = (bf16[2,128,4,64]{1,3,2,0:T(8,128)(2,1)S(1)}, bf16[2,128,4,64]{1,3,2,0:T(8,128)(2,1)}, u32[]{:S(2)}) copy-start(bf16[2,128,4,64]{1,3,2,0:T(8,128)(2,1)} %copy-done.17) | copy-start | bytes 393220
  140.8 2.9 %copy-start.11 = (f32[2,4,128,128]{2,3,1,0:T(8,128)S(1)}, f32[2,4,128,128]{2,3,1,0:T(8,128)}, u32[]{:S(2)}) copy-start(f32[2,4,128,128]{2,3,1,0:T(8,128)} %get-tuple-element.11) | copy-start | bytes 1572868
  142.3 1.7 copy-start.16
  144.0 1.0 copy-start.21
  145.0 8.3 %copy-start.6 = (bf16[8,48,256]{2,1,0:T(8,128)(2,1)S(1)}, bf16[8,48,256]{2,1,0:T(8,128)(2,1)}, u32[]{:S(2)}) copy-start(bf16[8,48,256]{2,1,0:T(8,128)(2,1)} %copy-done.5) | copy-start | bytes 589828
Sparse Core Ops, SparseCore 0:
  22.1 22.3 reduce-scatter.4
  94.7 24.1 reduce-scatter.8
  130.1 23.2 reduce-scatter.6
  155.8 21.6 reduce-scatter.10

commit v2 on v1

--- a/solution.py
+++ b/solution.py
@@ -1,6 +1,10 @@
+import functools
+
 import jax
 import jax.numpy as jnp
 from jax import lax
+from jax.experimental import pallas as pl
+from jax.experimental.pallas import tpu as pltpu
 from jax.sharding import PartitionSpec as P
 
 HEAD_DIM = 64
@@ -9,6 +13,342 @@
 
 norm_eps = 1e-06
 neg_fill = -1e30
+
+MESH = pl.DeviceIdType.MESH
+KEY_LANES = 128
+f32, bf16 = jnp.float32, jnp.bfloat16
+
+
+def dot(a, b):
+    return lax.dot_general(a, b, (((1,), (0,)), ((), ())), preferred_element_type=f32)
+
+
+def dot_nt(a, b):
+    return lax.dot_general(a, b, (((1,), (1,)), ((), ())), preferred_element_type=f32)
+
+
+def dot_tn(a, b):
+    return lax.dot_general(a, b, (((0,), (0,)), ((), ())), preferred_element_type=f32)
+
+
+def fused_kernel(
+    bands, cap,
+    cells, d_result, row_gain, col_gain, seg, dest, key, rw_any, ro_any, cw_any, co_any,
+    result, d_cells,
+    rw, ro, cw, co, xr, xc, dxc, dxr, e_out, e_in,
+    d_out_buf, m_out, s_out, g_out, s_back, g_back,
+    r_sib, r_got, r_x, r_xgot, c_sib, c_got, c_x, c_xgot,
+    b_sib, b_got, b_x, b_xgot, q_sib, q_got, q_x, q_xgot,
+    p_row, p_col, dn_row, dn_col,
+    w_sem, ag_send, ag_recv, rs_send, rs_recv, aa_send, aa_recv,
+):
+    rows, width = cells.shape
+    groups = xr.shape[0]
+    slots = bands * cap
+    heads = width // HEAD_DIM
+    features = groups * width
+    band, me = lax.axis_index("band"), lax.axis_index("mp")
+    near = me + 1 - 2 * lax.rem(me, 2)
+    far = lax.rem(me + 2, 4)
+    corner = lax.rem(near + 2, 4)
+    pending = []
+
+    loads = []
+    for i, (src, dst) in enumerate(((rw_any, rw), (ro_any, ro), (cw_any, cw), (co_any, co))):
+        load = pltpu.make_async_copy(src, dst, w_sem.at[i])
+        load.start()
+        loads.append(load)
+
+    xr[me] = cells[...]
+
+    barrier = pltpu.get_barrier_semaphore()
+    for peer in (near, far):
+        pl.semaphore_signal(barrier, inc=1, device_id=(band, peer), device_id_type=MESH)
+    for d in range(1, bands):
+        pl.semaphore_signal(
+            barrier, inc=1, device_id=(lax.rem(band + d, bands), me), device_id_type=MESH
+        )
+    pl.semaphore_wait(barrier, bands + 1)
+
+    def send(src, dst, send_sem, recv_sem, to):
+        copy = pltpu.make_async_remote_copy(
+            src_ref=src, dst_ref=dst, send_sem=send_sem, recv_sem=recv_sem,
+            device_id=to, device_id_type=MESH,
+        )
+        copy.start()
+        pending.append(copy)
+        return copy
+
+    def spread_start(buf, n):
+        across = send(buf.at[me], buf.at[me], ag_send.at[n, 0], ag_recv.at[n, 0], (band, far))
+        beside = send(buf.at[me], buf.at[me], ag_send.at[n, 1], ag_recv.at[n, 1], (band, near))
+        return across, beside
+
+    def spread_relay(buf, n, started):
+        across, beside = started
+        across.wait_recv()
+        relay = send(buf.at[far], buf.at[far], ag_send.at[n, 2], ag_recv.at[n, 2], (band, near))
+        return beside, relay
+
+    def spread_wait(copies):
+        for copy in copies:
+            copy.wait_recv()
+
+    def exchange_start(src, dst_at, n):
+        copies = []
+        for d in range(1, bands):
+            to = lax.rem(band + d, bands)
+            copies.append(
+                send(src.at[pl.ds(pl.multiple_of(to * cap, 16), cap)], dst_at(band),
+                     aa_send.at[n, d], aa_recv.at[n, d], (to, me))
+            )
+        dst_at(band)[...] = src[pl.ds(pl.multiple_of(band * cap, 16), cap), :]
+        return copies
+
+    def exchange_wait(copies):
+        for copy in copies:
+            copy.wait_recv()
+
+    def chunk(ref):
+        return lambda s: ref.at[pl.ds(pl.multiple_of(s * cap, 16), cap)]
+
+    def inner_chunk(ref):
+        return lambda s: ref.at[me, pl.ds(pl.multiple_of(s * cap, 16), cap)]
+
+    def sum_start(part, bufs, n):
+        sib, got, _, _ = bufs
+        sib[0] = part(corner).astype(bf16)
+        a = send(sib.at[0], got.at[0], rs_send.at[n, 0], rs_recv.at[n, 0], (band, near))
+        sib[1] = part(near).astype(bf16)
+        b = send(sib.at[1], got.at[1], rs_send.at[n, 1], rs_recv.at[n, 1], (band, near))
+        return a, b, part(far)
+
+    def sum_cross(bufs, n, state):
+        _, got, out, arrived = bufs
+        a, b, mine = state
+        a.wait_recv()
+        out[...] = (mine + got[0].astype(f32)).astype(bf16)
+        c = send(out, arrived, rs_send.at[n, 2], rs_recv.at[n, 2], (band, far))
+        return b, c
+
+    def sum_end(part, bufs, state):
+        _, got, _, arrived = bufs
+        b, c = state
+        own = part(me).astype(bf16).astype(f32)
+        b.wait_recv()
+        own = own + got[1].astype(f32)
+        c.wait_recv()
+        return own + arrived[...].astype(f32)
+
+    def lanes(c):
+        return pl.ds(pl.multiple_of(c * width, 128), width)
+
+    def project(x, gain, w):
+        total = jnp.zeros((x.shape[1], 1), f32)
+        for c in range(groups):
+            v = x[c].astype(f32)
+            total = total + jnp.sum(v * v, axis=-1, keepdims=True)
+        inv = lax.rsqrt(total / features + norm_eps)
+        acc = [None] * 3
+        for c in range(groups):
+            n = (x[c].astype(f32) * inv * gain[c]).astype(bf16)
+            for i in range(3):
+                t = dot(n, w[i, c * width:(c + 1) * width, :])
+                acc[i] = t if c == 0 else acc[i] + t
+        q, k, v = (t.astype(bf16) for t in acc)
+        return inv, q, k, v
+
+    head_of = lax.broadcasted_iota(jnp.int32, (1, width), 1) // HEAD_DIM
+
+    def only(h, t):
+        return jnp.where(head_of == h, t, jnp.zeros_like(t))
+
+    def attend(q, k, v, allowed, saved):
+        out = None
+        for h in range(heads):
+            s = dot_nt(only(h, q), k) * HEAD_DIM ** (-0.5)
+            s = jnp.where(allowed, s, neg_fill)
+            e = jnp.exp(s - jnp.max(s, axis=-1, keepdims=True))
+            p = e * (1.0 / jnp.sum(e, axis=-1, keepdims=True))
+            saved[h] = p
+            t = dot(p.astype(bf16), only(h, v))
+            out = t if h == 0 else out + t
+        return out.astype(bf16)
+
+    def back(x, dx, inv, gain, w, wo, q, k, v, saved, dn):
+        da = None
+        for c in range(groups):
+            t = dot_nt(dx[c], wo[:, c * width:(c + 1) * width])
+            da = t if c == 0 else da + t
+        da = da.astype(bf16)
+        dq = dk = dv = None
+        for h in range(heads):
+            dah = only(h, da)
+            p = saved[h]
+            dp = dot_nt(dah, v)
+            tv = dot_tn(p.astype(bf16), dah)
+            ds = p * (dp - jnp.sum(dp * p, axis=-1, keepdims=True))
+            ds = (ds * HEAD_DIM ** (-0.5)).astype(bf16)
+            tq = dot(ds, only(h, k))
+            tk = dot_tn(ds, only(h, q))
+            dq, dk, dv = (tq, tk, tv) if h == 0 else (dq + tq, dk + tk, dv + tv)
+        dq, dk, dv = dq.astype(bf16), dk.astype(bf16), dv.astype(bf16)
+        total = jnp.zeros((x.shape[1], 1), f32)
+        for c in range(groups):
+            at = slice(c * width, (c + 1) * width)
+            g = dot_nt(dq, w[0, at, :]) + dot_nt(dk, w[1, at, :]) + dot_nt(dv, w[2, at, :])
+            g = g.astype(bf16)
+            dn[c] = g
+            total = total + jnp.sum(x[c].astype(f32) * (g.astype(f32) * gain[c]), axis=-1, keepdims=True)
+        slope = inv * inv * inv * total * (1.0 / features)
+
+        def part(c):
+            return inv * (dn[c].astype(f32) * gain[c]) - x[c].astype(f32) * slope
+
+        return part
+
+    cells_out = spread_start(xr, 0)
+
+    down = lax.broadcasted_iota(jnp.int32, (rows, rows), 0)
+    over = lax.broadcasted_iota(jnp.int32, (rows, rows), 1)
+
+    def pair(ref):
+        along = jnp.broadcast_to(ref[...].astype(f32), (rows, rows))
+        return along, along.T
+
+    to_over, to_down = pair(dest)
+    same = to_over == to_down
+    rank_over = jnp.sum(jnp.where(same & (down < over), 1.0, 0.0), axis=0, keepdims=True)
+    slot_over = to_over[0:1, :] * cap + rank_over
+    at_slot = lax.broadcasted_iota(jnp.int32, (slots, rows), 0).astype(f32)
+    place = jnp.where(at_slot == slot_over, 1.0, 0.0).astype(bf16)
+    _, key_down = pair(key)
+    lane = lax.broadcasted_iota(jnp.int32, (rows, KEY_LANES), 1).astype(f32)
+    marks = jnp.where(key_down[:, :KEY_LANES] == lane, 1.0, 0.0).astype(bf16)
+    e_out[...] = dot(place, marks).astype(bf16)
+    d_out_buf[...] = dot(place, d_result[...]).astype(bf16)
+    early = exchange_start(d_out_buf, inner_chunk(dxc), 0)
+    early_keys = exchange_start(e_out, chunk(e_in), 1)
+
+    cells_out = spread_relay(xr, 0, cells_out)
+    seg_over, seg_down = pair(seg)
+    row_allowed = (seg_over == seg_down) & (down // TILE == over // TILE)
+    spread_wait(cells_out)
+
+    loads[0].wait()
+    row_inv, rq, rk, rv = project(xr, row_gain, rw)
+    exchange_wait(early)
+    exchange_wait(early_keys)
+    d_spread = spread_start(dxc, 1)
+    row_att = attend(rq, rk, rv, row_allowed, p_row)
+    loads[1].wait()
+
+    def row_term(c):
+        return dot(row_att, ro[:, lanes(c)])
+
+    bufs = (r_sib, r_got, r_x, r_xgot)
+    state = sum_start(row_term, bufs, 0)
+    d_spread = spread_relay(dxc, 1, d_spread)
+    state = sum_cross(bufs, 0, state)
+    mixed = (cells[...].astype(f32) + sum_end(row_term, bufs, state)).astype(bf16)
+    m_out[...] = dot(place, mixed).astype(bf16)
+    arriving = exchange_start(m_out, inner_chunk(xc), 2)
+
+    marks_in = e_in[...]
+    col_allowed = dot_nt(marks_in, marks_in) > 0.5
+    col_allowed = col_allowed | (
+        lax.broadcasted_iota(jnp.int32, (slots, slots), 0)
+        == lax.broadcasted_iota(jnp.int32, (slots, slots), 1)
+    )
+    loads[2].wait()
+    loads[3].wait()
+    exchange_wait(arriving)
+    col_spread = spread_start(xc, 2)
+    spread_wait(d_spread)
+    spread_wait(spread_relay(xc, 2, col_spread))
+
+    col_inv, cq, ck, cv = project(xc, col_gain, cw)
+    col_att = attend(cq, ck, cv, col_allowed, p_col)
+
+    def col_term(c):
+        return dot(col_att, co[:, lanes(c)])
+
+    fwd_bufs = (c_sib, c_got, c_x, c_xgot)
+    fwd = sum_start(col_term, fwd_bufs, 1)
+    fwd = sum_cross(fwd_bufs, 1, fwd)
+    col_part = back(xc, dxc, col_inv, col_gain, cw, co, cq, ck, cv, p_col, dn_col)
+    bwd_bufs = (b_sib, b_got, b_x, b_xgot)
+    bwd = sum_start(col_part, bwd_bufs, 2)
+    bwd = sum_cross(bwd_bufs, 2, bwd)
+    g_out[...] = (dxc[me].astype(f32) + sum_end(col_part, bwd_bufs, bwd)).astype(bf16)
+    g_copies = exchange_start(g_out, chunk(g_back), 3)
+    s_out[...] = (xc[me].astype(f32) + sum_end(col_term, fwd_bufs, fwd)).astype(bf16)
+    s_copies = exchange_start(s_out, chunk(s_back), 4)
+    exchange_wait(g_copies)
+    dxr[me] = dot_tn(place, g_back[...]).astype(bf16)
+    last = spread_start(dxr, 3)
+    exchange_wait(s_copies)
+    result[...] = dot_tn(place, s_back[...]).astype(bf16)
+    spread_wait(spread_relay(dxr, 3, last))
+
+    row_part = back(xr, dxr, row_inv, row_gain, rw, ro, rq, rk, rv, p_row, dn_row)
+    end_bufs = (q_sib, q_got, q_x, q_xgot)
+    end = sum_start(row_part, end_bufs, 3)
+    end = sum_cross(end_bufs, 3, end)
+    d_cells[...] = (dxr[me].astype(f32) + sum_end(row_part, end_bufs, end)).astype(bf16)
+    for copy in pending:
+        copy.wait_send()
+
+
+def fused(bands, cells, row_gain, row_qkv, row_out, col_gain, col_qkv, col_out, row_seg, col_dest, index, d_result):
+    rows, width = cells.shape
+    features = row_out.shape[1]
+    groups = features // width
+    heads = width // HEAD_DIM
+    cap = 3 * rows // (2 * bands)
+    slots = bands * cap
+    vmem = pl.BlockSpec(memory_space=pltpu.VMEM)
+    hbm = pl.BlockSpec(memory_space=pl.ANY)
+
+    def sum_bufs(n):
+        return [
+            pltpu.VMEM((2, n, width), bf16), pltpu.VMEM((2, n, width), bf16),
+            pltpu.VMEM((n, width), bf16), pltpu.VMEM((n, width), bf16),
+        ]
+
+    return pl.pallas_call(
+        functools.partial(fused_kernel, bands, cap),
+        out_shape=(
+            jax.ShapeDtypeStruct(cells.shape, bf16),
+            jax.ShapeDtypeStruct(cells.shape, bf16),
+        ),
+        in_specs=[vmem] * 7 + [hbm] * 4,
+        out_specs=(vmem, vmem),
+        scratch_shapes=[
+            pltpu.VMEM(row_qkv.shape, bf16), pltpu.VMEM(row_out.shape, bf16),
+            pltpu.VMEM(col_qkv.shape, bf16), pltpu.VMEM(col_out.shape, bf16),
+            pltpu.VMEM((groups, rows, width), bf16), pltpu.VMEM((groups, slots, width), bf16),
+            pltpu.VMEM((groups, slots, width), bf16), pltpu.VMEM((groups, rows, width), bf16),
+            pltpu.VMEM((slots, KEY_LANES), bf16), pltpu.VMEM((slots, KEY_LANES), bf16),
+            *[pltpu.VMEM((slots, width), bf16) for _ in range(6)],
+            *sum_bufs(rows), *sum_bufs(slots), *sum_bufs(slots), *sum_bufs(rows),
+            pltpu.VMEM((heads, rows, rows), f32), pltpu.VMEM((heads, slots, slots), f32),
+            pltpu.VMEM((groups, rows, width), bf16), pltpu.VMEM((groups, slots, width), bf16),
+            pltpu.SemaphoreType.DMA((4,)),
+            pltpu.SemaphoreType.DMA((4, 3)), pltpu.SemaphoreType.DMA((4, 3)),
+            pltpu.SemaphoreType.DMA((4, 3)), pltpu.SemaphoreType.DMA((4, 3)),
+            pltpu.SemaphoreType.DMA((5, bands)), pltpu.SemaphoreType.DMA((5, bands)),
+        ],
+        compiler_params=pltpu.CompilerParams(
+            collective_id=0, has_side_effects=True, vmem_limit_bytes=48 * 1024 * 1024
+        ),
+        cost_estimate=pl.CostEstimate(flops=8 * 10**9, bytes_accessed=5 * 10**6, transcendentals=10**6),
+    )(
+        cells, d_result,
+        row_gain.reshape(groups, 1, width), col_gain.reshape(groups, 1, width),
+        row_seg.reshape(1, rows), col_dest.reshape(1, rows), index.reshape(1, rows),
+        row_qkv, row_out, col_qkv, col_out,
+    )
 
 
 def block_terms(inputs, norm_gain, query_key_value_weight, w_out, allowed, tile_rows):
@@ -73,6 +413,12 @@
     band_count = lax.axis_size("band")
     capacity = max(2, 3 * cell_rows // (2 * band_count))
     slot_total = band_count * capacity
+    spare = (3 * cell_rows) % (2 * band_count) or capacity % 16
+    if lax.axis_size("mp") == 4 and cell_rows == 2 * TILE and not spare:
+        return fused(
+            band_count, cells, row_gain, row_qkv, row_out, col_gain, col_qkv, col_out,
+            row_seg, col_dest, sheet_column_index, d_result,
+        )
     gathered = widen(cells)
     row_groups = row_seg.reshape(cell_rows // TILE, TILE)
     row_mask = row_groups[:, :, None] == row_groups[:, None, :]

time: 188 us -> 83.9 us (0.45)
  the two profiles are of different devices: /device:TPU:12 before, /device:TPU:0 now
where the time goes in v2:
time: 83.9 us; the launch traced here: 83.5 us
  Pallas kernels  71.4 us (85%)
  local copies, waits for them, and re-layouts  11.4 us (14%)
    pallas_call x1, Pallas kernels, fused(): pl.pallas_call(functools.partial(fused_kernel, bands, cap), out_shape=(ja...  71.4 us
    unnamed x24, local copies, waits for them, and re-layouts  11.4 us

profile of v2, /device:TPU:0, one launch (start us, length us, event | category | flops | bytes accessed | tf_op | source)
XLA Modules:
  0.0 83.5 jit_solution(1367421947100230209)
XLA Ops:
  0.6 0.0 copy-start
  0.6 1.4 %copy-done = bf16[3,1024,256]{2,1,0:T(8,128)(2,1)S(1)} copy-done((bf16[3,1024,256]{2,1,0:T(8,128)(2,1)S(1)}, bf16[3,1024,256]{2,1,0:T(8,128)(2,1)}, u32[]{:S(2)}) %copy-start) | copy-done | bytes 1572888
  2.0 0.0 copy-start.1
  2.0 1.4 %copy-done.1 = bf16[3,1024,256]{2,1,0:T(8,128)(2,1)S(1)} copy-done((bf16[3,1024,256]{2,1,0:T(8,128)(2,1)S(1)}, bf16[3,1024,256]{2,1,0:T(8,128)(2,1)}, u32[]{:S(2)}) %copy-start.1) | copy-done | bytes 1572888
  3.5 0.0 copy-start.2
  3.5 1.0 %copy-done.2 = bf16[256,1024]{1,0:T(8,128)(2,1)S(1)} copy-done((bf16[256,1024]{1,0:T(8,128)(2,1)S(1)}, bf16[256,1024]{1,0:T(8,128)(2,1)}, u32[]{:S(2)}) %copy-start.2) | copy-done | bytes 524312
  4.5 0.0 copy-start.3
  4.5 1.0 %copy-done.3 = bf16[256,1024]{1,0:T(8,128)(2,1)S(1)} copy-done((bf16[256,1024]{1,0:T(8,128)(2,1)S(1)}, bf16[256,1024]{1,0:T(8,128)(2,1)}, u32[]{:S(2)}) %copy-start.3) | copy-done | bytes 524312
  5.5 0.0 copy-start.4
  5.5 0.9 %copy-done.4 = bf16[256,256]{1,0:T(8,128)(2,1)S(1)} copy-done((bf16[256,256]{1,0:T(8,128)(2,1)S(1)}, bf16[256,256]{1,0:T(8,128)(2,1)}, u32[]{:S(2)}) %copy-start.4) | copy-done | bytes 131096
  6.4 0.0 copy-start.5
  6.4 0.9 %copy-done.5 = bf16[256,256]{1,0:T(8,128)(2,1)S(1)} copy-done((bf16[256,256]{1,0:T(8,128)(2,1)S(1)}, bf16[256,256]{1,0:T(8,128)(2,1)}, u32[]{:S(2)}) %copy-start.5) | copy-done | bytes 131096
  7.3 0.0 copy-start.6
  7.3 0.7 copy-done.6
  8.0 0.0 copy-start.7
  8.0 0.7 copy-done.7
  8.7 0.0 copy-start.8
  8.7 0.7 copy-done.8
  9.4 0.0 copy-start.9
  9.4 0.7 copy-done.9
  10.1 0.0 copy-start.10
  10.1 0.7 copy-done.10
  10.8 71.4 %shard_map.122 = (bf16[256,256]{1,0:T(8,128)(2,1)S(1)}, bf16[256,256]{1,0:T(8,128)(2,1)S(1)}) custom-call(bf16[256,256]{1,0:T(8,128)(2,1)S(1)} %copy-done.4, bf16[256,256]{1,0:T(8,128)(2,1)S(1)} %copy-done.5, f32[4,1,256]{2,1,0:T(1,128)S(1)} %bitcast.5, f32[4,1,256]{2,1,0:T(1,128)S(1)} %bitcast.6, s32[1,256]{1,0:T(1,128)S(1)} %bitcast.7, ...), custom_call_target="tpu_custom_call" | custom-call | flops 8000000000 | bytes 5000000 | tf_op jit(solution)/shard_map/pallas_call | solution.py:319
  82.2 0.7 copy.15
  82.9 0.7 copy.16
Async XLA Ops:
  0.6 1.4 %copy-start = (bf16[3,1024,256]{2,1,0:T(8,128)(2,1)S(1)}, bf16[3,1024,256]{2,1,0:T(8,128)(2,1)}, u32[]{:S(2)}) copy-start(bf16[3,1024,256]{2,1,0:T(8,128)(2,1)} %rw_any.1) | copy-start | bytes 4718596
  2.0 1.4 %copy-start.1 = (bf16[3,1024,256]{2,1,0:T(8,128)(2,1)S(1)}, bf16[3,1024,256]{2,1,0:T(8,128)(2,1)}, u32[]{:S(2)}) copy-start(bf16[3,1024,256]{2,1,0:T(8,128)(2,1)} %cw_any.1) | copy-start | bytes 4718596
  3.5 1.0 %copy-start.2 = (bf16[256,1024]{1,0:T(8,128)(2,1)S(1)}, bf16[256,1024]{1,0:T(8,128)(2,1)}, u32[]{:S(2)}) copy-start(bf16[256,1024]{1,0:T(8,128)(2,1)} %ro_any.1) | copy-start | bytes 1572868
  4.5 1.0 %copy-start.3 = (bf16[256,1024]{1,0:T(8,128)(2,1)S(1)}, bf16[256,1024]{1,0:T(8,128)(2,1)}, u32[]{:S(2)}) copy-start(bf16[256,1024]{1,0:T(8,128)(2,1)} %co_any.1) | copy-start | bytes 1572868
  5.5 0.9 %copy-start.4 = (bf16[256,256]{1,0:T(8,128)(2,1)S(1)}, bf16[256,256]{1,0:T(8,128)(2,1)}, u32[]{:S(2)}) copy-start(bf16[256,256]{1,0:T(8,128)(2,1)} %cells.1) | copy-start | bytes 393220
  6.4 0.9 %copy-start.5 = (bf16[256,256]{1,0:T(8,128)(2,1)S(1)}, bf16[256,256]{1,0:T(8,128)(2,1)}, u32[]{:S(2)}) copy-start(bf16[256,256]{1,0:T(8,128)(2,1)} %d_result.1) | copy-start | bytes 393220
  7.3 0.7 copy-start.6
  8.0 0.7 copy-start.7
  8.7 0.7 copy-start.8
  9.4 0.7 copy-start.9
  10.1 0.7 copy-start.10

commit v3 on v2

--- a/solution.py
+++ b/solution.py
@@ -33,14 +33,14 @@
 
 def fused_kernel(
     bands, cap,
-    cells, d_result, row_gain, col_gain, seg, dest, key, rw_any, ro_any, cw_any, co_any,
+    cells, d_any, rg_any, cg_any, seg_any, dest_any, key_any, rw_any, ro_any, cw_any, co_any,
     result, d_cells,
-    rw, ro, cw, co, xr, xc, dxc, dxr, e_out, e_in,
+    d_result, row_gain, col_gain, seg, dest, key, rw, ro, cw, co, xr, xc, dxc, dxr, e_out, e_in,
     d_out_buf, m_out, s_out, g_out, s_back, g_back,
     r_sib, r_got, r_x, r_xgot, c_sib, c_got, c_x, c_xgot,
     b_sib, b_got, b_x, b_xgot, q_sib, q_got, q_x, q_xgot,
     p_row, p_col, dn_row, dn_col,
-    w_sem, ag_send, ag_recv, rs_send, rs_recv, aa_send, aa_recv,
+    w_sem, fw_send, fw_recv, ag_send, ag_recv, rs_send, rs_recv, aa_send, aa_recv,
 ):
     rows, width = cells.shape
     groups = xr.shape[0]
@@ -54,12 +54,13 @@
     pending = []
 
     loads = []
-    for i, (src, dst) in enumerate(((rw_any, rw), (ro_any, ro), (cw_any, cw), (co_any, co))):
+    for i, (src, dst) in enumerate((
+        (cells, xr.at[me]), (dest_any, dest), (key_any, key), (d_any, d_result), (seg_any, seg),
+        (rg_any, row_gain), (rw_any, rw), (ro_any, ro), (cg_any, col_gain), (cw_any, cw), (co_any, co),
+    )):
         load = pltpu.make_async_copy(src, dst, w_sem.at[i])
         load.start()
         loads.append(load)
-
-    xr[me] = cells[...]
 
     barrier = pltpu.get_barrier_semaphore()
     for peer in (near, far):
@@ -116,19 +117,15 @@
         return lambda s: ref.at[me, pl.ds(pl.multiple_of(s * cap, 16), cap)]
 
     def sum_start(part, bufs, n):
-        sib, got, _, _ = bufs
+        sib, got, out, arrived = bufs
         sib[0] = part(corner).astype(bf16)
         a = send(sib.at[0], got.at[0], rs_send.at[n, 0], rs_recv.at[n, 0], (band, near))
-        sib[1] = part(near).astype(bf16)
-        b = send(sib.at[1], got.at[1], rs_send.at[n, 1], rs_recv.at[n, 1], (band, near))
-        return a, b, part(far)
-
-    def sum_cross(bufs, n, state):
-        _, got, out, arrived = bufs
-        a, b, mine = state
+        mine = part(far)
         a.wait_recv()
         out[...] = (mine + got[0].astype(f32)).astype(bf16)
         c = send(out, arrived, rs_send.at[n, 2], rs_recv.at[n, 2], (band, far))
+        sib[1] = part(near).astype(bf16)
+        b = send(sib.at[1], got.at[1], rs_send.at[n, 1], rs_recv.at[n, 1], (band, near))
         return b, c
 
     def sum_end(part, bufs, state):
@@ -207,6 +204,7 @@
 
         return part
 
+    loads[0].wait()
     cells_out = spread_start(xr, 0)
 
     down = lax.broadcasted_iota(jnp.int32, (rows, rows), 0)
@@ -216,6 +214,8 @@
         along = jnp.broadcast_to(ref[...].astype(f32), (rows, rows))
         return along, along.T
 
+    for i in (1, 2, 3, 4):
+        loads[i].wait()
     to_over, to_down = pair(dest)
     same = to_over == to_down
     rank_over = jnp.sum(jnp.where(same & (down < over), 1.0, 0.0), axis=0, keepdims=True)
@@ -235,13 +235,14 @@
     row_allowed = (seg_over == seg_down) & (down // TILE == over // TILE)
     spread_wait(cells_out)
 
-    loads[0].wait()
+    loads[5].wait()
+    loads[6].wait()
     row_inv, rq, rk, rv = project(xr, row_gain, rw)
     exchange_wait(early)
     exchange_wait(early_keys)
     d_spread = spread_start(dxc, 1)
     row_att = attend(rq, rk, rv, row_allowed, p_row)
-    loads[1].wait()
+    loads[7].wait()
 
     def row_term(c):
         return dot(row_att, ro[:, lanes(c)])
@@ -249,8 +250,7 @@
     bufs = (r_sib, r_got, r_x, r_xgot)
     state = sum_start(row_term, bufs, 0)
     d_spread = spread_relay(dxc, 1, d_spread)
-    state = sum_cross(bufs, 0, state)
-    mixed = (cells[...].astype(f32) + sum_end(row_term, bufs, state)).astype(bf16)
+    mixed = (xr[me].astype(f32) + sum_end(row_term, bufs, state)).astype(bf16)
     m_out[...] = dot(place, mixed).astype(bf16)
     arriving = exchange_start(m_out, inner_chunk(xc), 2)
 
@@ -260,12 +260,26 @@
         lax.broadcasted_iota(jnp.int32, (slots, slots), 0)
         == lax.broadcasted_iota(jnp.int32, (slots, slots), 1)
     )
-    loads[2].wait()
-    loads[3].wait()
-    exchange_wait(arriving)
-    col_spread = spread_start(xc, 2)
+    for i in (8, 9, 10):
+        loads[i].wait()
+    moved = []
+    for d in range(bands):
+        if d:
+            arriving[d - 1].wait_recv()
+        at = pl.ds(pl.multiple_of(lax.rem(band + bands - d, bands) * cap, 16), cap)
+        mine = xc.at[me, at]
+        across = send(mine, mine, fw_send.at[d, 0], fw_recv.at[d, 0], (band, far))
+        beside = send(mine, mine, fw_send.at[d, 1], fw_recv.at[d, 1], (band, near))
+        moved.append((at, across, beside))
     spread_wait(d_spread)
-    spread_wait(spread_relay(xc, 2, col_spread))
+    relays = []
+    for d, (at, across, _) in enumerate(moved):
+        across.wait_recv()
+        theirs = xc.at[far, at]
+        relays.append(send(theirs, theirs, fw_send.at[d, 2], fw_recv.at[d, 2], (band, near)))
+    for _, _, beside in moved:
+        beside.wait_recv()
+    spread_wait(relays)
 
     col_inv, cq, ck, cv = project(xc, col_gain, cw)
     col_att = attend(cq, ck, cv, col_allowed, p_col)
@@ -275,11 +289,9 @@
 
     fwd_bufs = (c_sib, c_got, c_x, c_xgot)
     fwd = sum_start(col_term, fwd_bufs, 1)
-    fwd = sum_cross(fwd_bufs, 1, fwd)
     col_part = back(xc, dxc, col_inv, col_gain, cw, co, cq, ck, cv, p_col, dn_col)
     bwd_bufs = (b_sib, b_got, b_x, b_xgot)
     bwd = sum_start(col_part, bwd_bufs, 2)
-    bwd = sum_cross(bwd_bufs, 2, bwd)
     g_out[...] = (dxc[me].astype(f32) + sum_end(col_part, bwd_bufs, bwd)).astype(bf16)
     g_copies = exchange_start(g_out, chunk(g_back), 3)
     s_out[...] = (xc[me].astype(f32) + sum_end(col_term, fwd_bufs, fwd)).astype(bf16)
@@ -294,7 +306,6 @@
     row_part = back(xr, dxr, row_inv, row_gain, rw, ro, rq, rk, rv, p_row, dn_row)
     end_bufs = (q_sib, q_got, q_x, q_xgot)
     end = sum_start(row_part, end_bufs, 3)
-    end = sum_cross(end_bufs, 3, end)
     d_cells[...] = (dxr[me].astype(f32) + sum_end(row_part, end_bufs, end)).astype(bf16)
     for copy in pending:
         copy.wait_send()
@@ -308,7 +319,7 @@
     cap = 3 * rows // (2 * bands)
     slots = bands * cap
     vmem = pl.BlockSpec(memory_space=pltpu.VMEM)
-    hbm = pl.BlockSpec(memory_space=pl.ANY)
+    hbm = pl.BlockSpec(memory_space=pltpu.HBM)
 
     def sum_bufs(n):
         return [
@@ -322,9 +333,12 @@
             jax.ShapeDtypeStruct(cells.shape, bf16),
             jax.ShapeDtypeStruct(cells.shape, bf16),
         ),
-        in_specs=[vmem] * 7 + [hbm] * 4,
+        in_specs=[hbm] * 11,
         out_specs=(vmem, vmem),
         scratch_shapes=[
+            pltpu.VMEM(d_result.shape, bf16),
+            pltpu.VMEM((groups, 1, width), f32), pltpu.VMEM((groups, 1, width), f32),
+            *[pltpu.VMEM((1, rows), jnp.int32) for _ in range(3)],
             pltpu.VMEM(row_qkv.shape, bf16), pltpu.VMEM(row_out.shape, bf16),
             pltpu.VMEM(col_qkv.shape, bf16), pltpu.VMEM(col_out.shape, bf16),
             pltpu.VMEM((groups, rows, width), bf16), pltpu.VMEM((groups, slots, width), bf16),
@@ -334,13 +348,14 @@
             *sum_bufs(rows), *sum_bufs(slots), *sum_bufs(slots), *sum_bufs(rows),
             pltpu.VMEM((heads, rows, rows), f32), pltpu.VMEM((heads, slots, slots), f32),
             pltpu.VMEM((groups, rows, width), bf16), pltpu.VMEM((groups, slots, width), bf16),
-            pltpu.SemaphoreType.DMA((4,)),
+            pltpu.SemaphoreType.DMA((11,)),
+            pltpu.SemaphoreType.DMA((bands, 3)), pltpu.SemaphoreType.DMA((bands, 3)),
             pltpu.SemaphoreType.DMA((4, 3)), pltpu.SemaphoreType.DMA((4, 3)),
             pltpu.SemaphoreType.DMA((4, 3)), pltpu.SemaphoreType.DMA((4, 3)),
             pltpu.SemaphoreType.DMA((5, bands)), pltpu.SemaphoreType.DMA((5, bands)),
         ],
         compiler_params=pltpu.CompilerParams(
-            collective_id=0, has_side_effects=True, vmem_limit_bytes=48 * 1024 * 1024
+            collective_id=0, has_side_effects=True, vmem_limit_bytes=60 * 1024 * 1024
         ),
         cost_estimate=pl.CostEstimate(flops=8 * 10**9, bytes_accessed=5 * 10**6, transcendentals=10**6),
     )(

time: 83.9 us -> 76 us (0.906)
  the two profiles are of different devices: /device:TPU:0 before, /device:TPU:12 now
where the time goes in v3:
time: 76 us; the launch traced here: 75.8 us
  Pallas kernels  72 us (95%)
  local copies, waits for them, and re-layouts  3.14 us (4%)
    pallas_call x1, Pallas kernels, fused(): pl.pallas_call(functools.partial(fused_kernel, bands, cap), out_shape=(ja...  72 us
    unnamed x2, local copies, waits for them, and re-layouts  3.14 us

profile of v3, /device:TPU:12, one launch (start us, length us, event | category | flops | bytes accessed | tf_op | source)
XLA Modules:
  0.0 75.8 jit_solution(3679653988751208772)
XLA Ops:
  0.6 72.0 %shard_map.122 = (bf16[256,256]{1,0:T(8,128)(2,1)}, bf16[256,256]{1,0:T(8,128)(2,1)}) custom-call(bf16[256,256]{1,0:T(8,128)(2,1)} %cells.1, bf16[256,256]{1,0:T(8,128)(2,1)} %d_any.1, f32[4,1,256]{2,1,0:T(1,128)} %bitcast.5, f32[4,1,256]{2,1,0:T(1,128)} %bitcast.6, s32[1,256]{1,0:T(1,128)} %bitcast.7, s32[1,256]{1,0:T(1,128)} %bitcast.8, s32[1,256]{1,0:T(1,128)} %bitcast.9, ...), custom_call_target="tpu_custom_call" | custom-call | flops 8000000000 | bytes 5000000 | tf_op jit(solution)/shard_map/pallas_call | solution.py:330
  72.7 1.6 %copy.15 = bf16[256,256]{1,0:T(8,128)(2,1)} copy(bf16[256,256]{1,0:T(8,128)(2,1)} %get-tuple-element.4) | data formatting | bytes 262144
  74.2 1.6 %copy.16 = bf16[256,256]{1,0:T(8,128)(2,1)} copy(bf16[256,256]{1,0:T(8,128)(2,1)} %get-tuple-element.5) | data formatting | bytes 262144

commit v4 on v3

--- a/solution.py
+++ b/solution.py
@@ -91,6 +91,21 @@
         relay = send(buf.at[far], buf.at[far], ag_send.at[n, 2], ag_recv.at[n, 2], (band, near))
         return beside, relay
 
+    def nothing():
+        return None
+
+    def arrival(buf, n, started):
+        across, beside = started
+        held = []
+
+        def cross():
+            held.append(spread_relay(buf, n, started)[1])
+
+        def turn():
+            held[0].wait_recv()
+
+        return ((me, nothing), (near, beside.wait_recv), (far, cross), (corner, turn))
+
     def spread_wait(copies):
         for copy in copies:
             copy.wait_recv()
@@ -117,9 +132,15 @@
         return lambda s: ref.at[me, pl.ds(pl.multiple_of(s * cap, 16), cap)]
 
     def sum_start(part, bufs, n):
+        return sum_cross(part, bufs, n, sum_open(part, bufs, n))
+
+    def sum_open(part, bufs, n):
+        sib, got, _, _ = bufs
+        sib[0] = part(corner).astype(bf16)
+        return send(sib.at[0], got.at[0], rs_send.at[n, 0], rs_recv.at[n, 0], (band, near))
+
+    def sum_cross(part, bufs, n, a):
         sib, got, out, arrived = bufs
-        sib[0] = part(corner).astype(bf16)
-        a = send(sib.at[0], got.at[0], rs_send.at[n, 0], rs_recv.at[n, 0], (band, near))
         mine = part(far)
         a.wait_recv()
         out[...] = (mine + got[0].astype(f32)).astype(bf16)
@@ -140,19 +161,22 @@
     def lanes(c):
         return pl.ds(pl.multiple_of(c * width, 128), width)
 
-    def project(x, gain, w):
+    def features_of(c):
+        return pl.ds(pl.multiple_of(c * width, 128), width)
+
+    def project(x, gain, w, order):
         total = jnp.zeros((x.shape[1], 1), f32)
-        for c in range(groups):
+        acc = [None] * 3
+        for c, ready in order:
+            ready()
             v = x[c].astype(f32)
+            n = (v * gain[c]).astype(bf16)
+            for i in range(3):
+                t = dot(n, w[i, features_of(c), :])
+                acc[i] = t if acc[i] is None else acc[i] + t
             total = total + jnp.sum(v * v, axis=-1, keepdims=True)
         inv = lax.rsqrt(total / features + norm_eps)
-        acc = [None] * 3
-        for c in range(groups):
-            n = (x[c].astype(f32) * inv * gain[c]).astype(bf16)
-            for i in range(3):
-                t = dot(n, w[i, c * width:(c + 1) * width, :])
-                acc[i] = t if c == 0 else acc[i] + t
-        q, k, v = (t.astype(bf16) for t in acc)
+        q, k, v = ((t * inv).astype(bf16) for t in acc)
         return inv, q, k, v
 
     head_of = lax.broadcasted_iota(jnp.int32, (1, width), 1) // HEAD_DIM
@@ -172,11 +196,12 @@
             out = t if h == 0 else out + t
         return out.astype(bf16)
 
-    def back(x, dx, inv, gain, w, wo, q, k, v, saved, dn):
+    def back(x, dx, inv, gain, w, wo, q, k, v, saved, dn, order, between):
         da = None
-        for c in range(groups):
-            t = dot_nt(dx[c], wo[:, c * width:(c + 1) * width])
-            da = t if c == 0 else da + t
+        for c, ready in order:
+            ready()
+            t = dot_nt(dx[c], wo[:, lanes(c)])
+            da = t if da is None else da + t
         da = da.astype(bf16)
         dq = dk = dv = None
         for h in range(heads):
@@ -189,6 +214,8 @@
             tq = dot(ds, only(h, k))
             tk = dot_tn(ds, only(h, q))
             dq, dk, dv = (tq, tk, tv) if h == 0 else (dq + tq, dk + tk, dv + tv)
+            if h == 1:
+                between()
         dq, dk, dv = dq.astype(bf16), dk.astype(bf16), dv.astype(bf16)
         total = jnp.zeros((x.shape[1], 1), f32)
         for c in range(groups):
@@ -230,14 +257,12 @@
     early = exchange_start(d_out_buf, inner_chunk(dxc), 0)
     early_keys = exchange_start(e_out, chunk(e_in), 1)
 
-    cells_out = spread_relay(xr, 0, cells_out)
     seg_over, seg_down = pair(seg)
     row_allowed = (seg_over == seg_down) & (down // TILE == over // TILE)
-    spread_wait(cells_out)
 
     loads[5].wait()
     loads[6].wait()
-    row_inv, rq, rk, rv = project(xr, row_gain, rw)
+    row_inv, rq, rk, rv = project(xr, row_gain, rw, arrival(xr, 0, cells_out))
     exchange_wait(early)
     exchange_wait(early_keys)
     d_spread = spread_start(dxc, 1)
@@ -273,23 +298,41 @@
         moved.append((at, across, beside))
     spread_wait(d_spread)
     relays = []
-    for d, (at, across, _) in enumerate(moved):
-        across.wait_recv()
-        theirs = xc.at[far, at]
-        relays.append(send(theirs, theirs, fw_send.at[d, 2], fw_recv.at[d, 2], (band, near)))
-    for _, _, beside in moved:
-        beside.wait_recv()
-    spread_wait(relays)
-
-    col_inv, cq, ck, cv = project(xc, col_gain, cw)
+
+    def all_near():
+        for _, _, beside in moved:
+            beside.wait_recv()
+
+    def all_far():
+        for d, (at, across, _) in enumerate(moved):
+            across.wait_recv()
+            theirs = xc.at[far, at]
+            relays.append(
+                send(theirs, theirs, fw_send.at[d, 2], fw_recv.at[d, 2], (band, near))
+            )
+
+    def all_corner():
+        spread_wait(relays)
+
+    col_inv, cq, ck, cv = project(
+        xc, col_gain, cw, ((me, nothing), (near, all_near), (far, all_far), (corner, all_corner))
+    )
     col_att = attend(cq, ck, cv, col_allowed, p_col)
 
     def col_term(c):
         return dot(col_att, co[:, lanes(c)])
 
     fwd_bufs = (c_sib, c_got, c_x, c_xgot)
-    fwd = sum_start(col_term, fwd_bufs, 1)
-    col_part = back(xc, dxc, col_inv, col_gain, cw, co, cq, ck, cv, p_col, dn_col)
+    first = sum_open(col_term, fwd_bufs, 1)
+    fwd = []
+
+    def between():
+        fwd.extend(sum_cross(col_term, fwd_bufs, 1, first))
+
+    landed = tuple((c, nothing) for c in range(groups))
+    col_part = back(
+        xc, dxc, col_inv, col_gain, cw, co, cq, ck, cv, p_col, dn_col, landed, between
+    )
     bwd_bufs = (b_sib, b_got, b_x, b_xgot)
     bwd = sum_start(col_part, bwd_bufs, 2)
     g_out[...] = (dxc[me].astype(f32) + sum_end(col_part, bwd_bufs, bwd)).astype(bf16)
@@ -299,11 +342,16 @@
     exchange_wait(g_copies)
     dxr[me] = dot_tn(place, g_back[...]).astype(bf16)
     last = spread_start(dxr, 3)
-    exchange_wait(s_copies)
-    result[...] = dot_tn(place, s_back[...]).astype(bf16)
-    spread_wait(spread_relay(dxr, 3, last))
-
-    row_part = back(xr, dxr, row_inv, row_gain, rw, ro, rq, rk, rv, p_row, dn_row)
+
+    def write_result():
+        exchange_wait(s_copies)
+        result[...] = dot_tn(place, s_back[...]).astype(bf16)
+
+
+    row_part = back(
+        xr, dxr, row_inv, row_gain, rw, ro, rq, rk, rv, p_row, dn_row,
+        arrival(dxr, 3, last), write_result,
+    )
     end_bufs = (q_sib, q_got, q_x, q_xgot)
     end = sum_start(row_part, end_bufs, 3)
     d_cells[...] = (dxr[me].astype(f32) + sum_end(row_part, end_bufs, end)).astype(bf16)

time: 76 us -> 75.3 us (level)
  no operation moved by 1% of the time
where the time goes in v4:
time: 75.3 us; the launch traced here: 75.1 us
  Pallas kernels  71.3 us (95%)
  local copies, waits for them, and re-layouts  3.14 us (4%)
    pallas_call x1, Pallas kernels, fused(): pl.pallas_call(functools.partial(fused_kernel, bands, cap), out_shape=(ja...  71.3 us
    unnamed x2, local copies, waits for them, and re-layouts  3.14 us

profile of v4, /device:TPU:12, one launch (start us, length us, event | category | flops | bytes accessed | tf_op | source)
XLA Modules:
  0.0 75.1 jit_solution(4064188566031012251)
XLA Ops:
  0.6 71.3 %shard_map.122 = (bf16[256,256]{1,0:T(8,128)(2,1)}, bf16[256,256]{1,0:T(8,128)(2,1)}) custom-call(bf16[256,256]{1,0:T(8,128)(2,1)} %cells.1, bf16[256,256]{1,0:T(8,128)(2,1)} %d_any.1, f32[4,1,256]{2,1,0:T(1,128)} %bitcast.5, f32[4,1,256]{2,1,0:T(1,128)} %bitcast.6, s32[1,256]{1,0:T(1,128)} %bitcast.7, s32[1,256]{1,0:T(1,128)} %bitcast.8, s32[1,256]{1,0:T(1,128)} %bitcast.9, ...), custom_call_target="tpu_custom_call" | custom-call | flops 8000000000 | bytes 5000000 | tf_op jit(solution)/shard_map/pallas_call | solution.py:378
  72.0 1.6 %copy.15 = bf16[256,256]{1,0:T(8,128)(2,1)} copy(bf16[256,256]{1,0:T(8,128)(2,1)} %get-tuple-element.4) | data formatting | bytes 262144
  73.6 1.6 %copy.16 = bf16[256,256]{1,0:T(8,128)(2,1)} copy(bf16[256,256]{1,0:T(8,128)(2,1)} %get-tuple-element.5) | data formatting | bytes 262144

commit v5 on v4

--- a/solution.py
+++ b/solution.py
@@ -34,7 +34,7 @@
 def fused_kernel(
     bands, cap,
     cells, d_any, rg_any, cg_any, seg_any, dest_any, key_any, rw_any, ro_any, cw_any, co_any,
-    result, d_cells,
+    both,
     d_result, row_gain, col_gain, seg, dest, key, rw, ro, cw, co, xr, xc, dxc, dxr, e_out, e_in,
     d_out_buf, m_out, s_out, g_out, s_back, g_back,
     r_sib, r_got, r_x, r_xgot, c_sib, c_got, c_x, c_xgot,
@@ -345,7 +345,7 @@
 
     def write_result():
         exchange_wait(s_copies)
-        result[...] = dot_tn(place, s_back[...]).astype(bf16)
+        both[0] = dot_tn(place, s_back[...]).astype(bf16)
 
 
     row_part = back(
@@ -354,7 +354,7 @@
     )
     end_bufs = (q_sib, q_got, q_x, q_xgot)
     end = sum_start(row_part, end_bufs, 3)
-    d_cells[...] = (dxr[me].astype(f32) + sum_end(row_part, end_bufs, end)).astype(bf16)
+    both[1] = (dxr[me].astype(f32) + sum_end(row_part, end_bufs, end)).astype(bf16)
     for copy in pending:
         copy.wait_send()
 
@@ -375,14 +375,11 @@
             pltpu.VMEM((n, width), bf16), pltpu.VMEM((n, width), bf16),
         ]
 
-    return pl.pallas_call(
+    both = pl.pallas_call(
         functools.partial(fused_kernel, bands, cap),
-        out_shape=(
-            jax.ShapeDtypeStruct(cells.shape, bf16),
-            jax.ShapeDtypeStruct(cells.shape, bf16),
-        ),
+        out_shape=jax.ShapeDtypeStruct((2, *cells.shape), bf16),
         in_specs=[hbm] * 11,
-        out_specs=(vmem, vmem),
+        out_specs=vmem,
         scratch_shapes=[
             pltpu.VMEM(d_result.shape, bf16),
             pltpu.VMEM((groups, 1, width), f32), pltpu.VMEM((groups, 1, width), f32),
@@ -412,6 +409,7 @@
         row_seg.reshape(1, rows), col_dest.reshape(1, rows), index.reshape(1, rows),
         row_qkv, row_out, col_qkv, col_out,
     )
+    return both[0], both[1]
 
 
 def block_terms(inputs, norm_gain, query_key_value_weight, w_out, allowed, tile_rows):

time: 75.3 us -> 73.8 us (0.980)
  local copies, waits for them, and re-layouts: 3.14 us -> 1.68 us
    unnamed x2 -> x0, local copies, waits for them, and re-layouts: 3.14 us -> none
    squeeze x0 -> x1, local copies, waits for them, and re-layouts: none -> 1.68 us  [fused(): return (both[0], both[1])]
where the time goes in v5:
time: 73.8 us; the launch traced here: 73.7 us
  Pallas kernels  71.3 us (97%)
  local copies, waits for them, and re-layouts  1.68 us (2%)
    pallas_call x1, Pallas kernels, fused(): pl.pallas_call(functools.partial(fused_kernel, bands, cap), out_shape=jax...  71.3 us
    squeeze x1, local copies, waits for them, and re-layouts, fused(): return (both[0], both[1])  1.68 us

profile of v5, /device:TPU:12, one launch (start us, length us, event | category | flops | bytes accessed | tf_op | source)
XLA Modules:
  0.0 73.7 jit_solution(294780195401759399)
XLA Ops:
  0.6 71.3 %shard_map.122 = bf16[2,256,256]{2,1,0:T(8,128)(2,1)} custom-call(bf16[256,256]{1,0:T(8,128)(2,1)} %cells.1, bf16[256,256]{1,0:T(8,128)(2,1)} %d_any.1, f32[4,1,256]{2,1,0:T(1,128)} %bitcast.9, f32[4,1,256]{2,1,0:T(1,128)} %bitcast.10, s32[1,256]{1,0:T(1,128)} %bitcast.11, s32[1,256]{1,0:T(1,128)} %bitcast.12, s32[1,256]{1,0:T(1,128)} %bitcast.13, ...), custom_call_target="tpu_custom_call" | custom-call | flops 8000000000 | bytes 5000000 | tf_op jit(solution)/shard_map/pallas_call | solution.py:378
  72.0 1.7 %slice_bitcast_fusion = (bf16[256,256]{1,0:T(8,128)(2,1)}, bf16[256,256]{1,0:T(8,128)(2,1)}) fusion(bf16[2,256,256]{2,1,0:T(8,128)(2,1)} %shard_map.122), kind=kLoop, calls=%fused_computation | loop fusion | bytes 524288 | tf_op jit(solution)/shard_map/squeeze | solution.py:412
